TPU v7x, 256 devices: a whole 4x4x8 slice. The times are simulated.
256 devices in a mesh: lon: 32 (over z, x_lo, core), lat: 8 (over y, x_hi).
Axes of the slice: x: 4 (x_hi: 2, x_lo: 2; x = x_hi * 2 + x_lo), y: 4, z: 8, core: 2. Of those that a mesh axis runs over, the one named last changes fastest.
Arguments:
- latents: bfloat16 [4, 96, 192, 1024], P(None, 'lat', 'lon'), may hold values from -6 to 6
- qkv_weight: bfloat16 [1024, 3072], replicated, may hold values from -0.1875 to 0.1875
- proj_weight: bfloat16 [1024, 1024], replicated, may hold values from -0.1875 to 0.1875
- merge_weight: bfloat16 [4096, 2048], P('lon'), may hold values from -0.09375 to 0.09375
- bias_table: float32 [16, 759], replicated, may hold values from -4 to 310
- bias_index: int32 [144, 144], replicated, may hold values from 0 to 758
- cotangent: bfloat16 [4, 48, 96, 2048], P(None, 'lat', 'lon'), may hold values from -6 to 6
Outputs:
- merged: bfloat16 [4, 48, 96, 2048], P(None, 'lat', 'lon')
- grad_latents: bfloat16 [4, 96, 192, 1024], P(None, 'lat', 'lon')
- grad_bias: float32 [16, 759], replicated
All inputs are finite; a program needn't handle non-finite values.
Results may differ from a plain program's by a relative error of at most 0.02.
Values may be sent and summed in bfloat16 or wider, within the bound.
A program may use at most 128 MiB of HBM per device.

v0:
```python
import jax
import jax.numpy as jnp
from jax import lax
from jax.sharding import PartitionSpec as P

WIN_LEV = 2
WIN_LAT = 12
WIN_LON = 6


EPS = 1e-05
MASKED = -1e30


def from_behind(shard, axis, by):
    devices = lax.axis_size(axis)
    return lax.ppermute(shard, axis, [(i, (i + by) % devices) for i in range(devices)])


def normalize(values):
    average = jnp.mean(values, axis=-1, keepdims=True)
    centered = values - average
    variance = jnp.mean(centered * centered, axis=-1, keepdims=True)
    return centered * lax.rsqrt(variance + EPS)


def to_windows(grid_cells):
    level_count, lat_rows, lon_cols, features = grid_cells.shape
    shaped = grid_cells.reshape(
        level_count // WIN_LEV,
        WIN_LEV,
        lat_rows // WIN_LAT,
        WIN_LAT,
        lon_cols // WIN_LON,
        WIN_LON,
        features,
    )
    shaped = shaped.transpose(0, 2, 4, 1, 3, 5, 6)
    return shaped.reshape(-1, WIN_LEV * WIN_LAT * WIN_LON, features)


def from_windows(window_rows, level_count, lat_rows, lon_cols):
    features = window_rows.shape[-1]
    shaped = window_rows.reshape(
        level_count // WIN_LEV,
        lat_rows // WIN_LAT,
        lon_cols // WIN_LON,
        WIN_LEV,
        WIN_LAT,
        WIN_LON,
        features,
    )
    shaped = shaped.transpose(0, 3, 1, 4, 2, 5, 6)
    return shaped.reshape(level_count, lat_rows, lon_cols, features)


def lat_regions(row_ids, total_rows):
    return jnp.where(
        row_ids < total_rows - WIN_LAT, 0, jnp.where(row_ids < total_rows - WIN_LAT // 2, 1, 2)
    ).astype(jnp.int32)


def region_labels(lat_ids, level_count, lon_cols):
    level_ids = jnp.arange(level_count, dtype=jnp.int32)
    region_ids = jnp.where(
        level_ids < level_count - WIN_LEV,
        0,
        jnp.where(level_ids < level_count - WIN_LEV // 2, 1, 2),
    ).astype(jnp.int32)
    labels = lat_ids[None, :, None] * 3 + region_ids[:, None, None]
    return jnp.broadcast_to(labels, (level_count, lat_ids.shape[0], lon_cols))


def attend(window_rows, window_labels, bias_table, bias_index, qkv_weight, proj_weight):
    num_windows, window_size, features = window_rows.shape
    head_count = bias_table.shape[0]
    head_dim = features // head_count
    flat_rows = window_rows.reshape(num_windows * window_size, features)
    normed = normalize(flat_rows.astype(jnp.float32)).astype(jnp.bfloat16)
    packed = jnp.dot(normed, qkv_weight, preferred_element_type=jnp.float32).astype(jnp.bfloat16)
    packed = packed.reshape(num_windows, window_size, 3, head_count, head_dim)
    scores = jnp.einsum(
        "wqhd,wkhd->whqk", packed[:, :, 0], packed[:, :, 1], preferred_element_type=jnp.float32
    ) * head_dim ** (-0.5)
    bias_terms = jnp.take(bias_table, bias_index, axis=1)
    allowed = window_labels[:, None, :, None] == window_labels[:, None, None, :]
    scores = jnp.where(allowed, scores + bias_terms[None], MASKED)
    row_max = jnp.max(scores, axis=-1, keepdims=True)
    weights = jnp.exp(scores - row_max)
    probabilities = (weights / jnp.sum(weights, axis=-1, keepdims=True)).astype(jnp.bfloat16)
    mixed_rows = jnp.einsum(
        "whqk,wkhd->wqhd", probabilities, packed[:, :, 2], preferred_element_type=jnp.float32
    ).astype(jnp.bfloat16)
    mixed_rows = mixed_rows.reshape(num_windows * window_size, features)
    block_out = flat_rows.astype(jnp.float32) + jnp.dot(
        mixed_rows, proj_weight, preferred_element_type=jnp.float32
    )
    return block_out.astype(jnp.bfloat16).reshape(num_windows, window_size, features)


def merge_inputs(grid_cells):
    level_count, lat_rows, lon_cols, features = grid_cells.shape
    shaped = grid_cells.reshape(level_count, lat_rows // 2, 2, lon_cols // 2, 2, features)
    shaped = shaped.transpose(0, 1, 3, 4, 2, 5)
    shaped = shaped.reshape(level_count * (lat_rows // 2) * (lon_cols // 2), 4 * features)
    return normalize(shaped.astype(jnp.float32)).astype(jnp.bfloat16)


def roll_forward(grid_cells):
    lat_shift = WIN_LAT // 2
    lon_shift = WIN_LON // 2
    grid_cells = jnp.roll(grid_cells, -(WIN_LEV // 2), axis=0)
    incoming = from_behind(grid_cells[:, :lat_shift], "lat", -1)
    grid_cells = jnp.concatenate([grid_cells[:, lat_shift:], incoming], axis=1)
    incoming = from_behind(grid_cells[:, :, :lon_shift], "lon", -1)
    return jnp.concatenate([grid_cells[:, :, lon_shift:], incoming], axis=2)


def roll_back(grid_cells):
    lat_shift = WIN_LAT // 2
    lon_shift = WIN_LON // 2
    lat_rows = grid_cells.shape[1]
    lon_cols = grid_cells.shape[2]
    incoming = from_behind(grid_cells[:, :, lon_cols - lon_shift :], "lon", 1)
    grid_cells = jnp.concatenate([incoming, grid_cells[:, :, : lon_cols - lon_shift]], axis=2)
    incoming = from_behind(grid_cells[:, lat_rows - lat_shift :], "lat", 1)
    grid_cells = jnp.concatenate([incoming, grid_cells[:, : lat_rows - lat_shift]], axis=1)
    return jnp.roll(grid_cells, WIN_LEV // 2, axis=0)


def shards(latents, qkv_weight, proj_weight, merge_weight, bias_table, bias_index, cotangent):
    level_count, lat_rows, lon_cols, features = latents.shape
    out_width = cotangent.shape[-1]
    total_rows = lat_rows * lax.axis_size("lat")
    global_rows = lax.axis_index("lat") * lat_rows + jnp.arange(lat_rows, dtype=jnp.int32)
    labels = region_labels(lat_regions(global_rows, total_rows), level_count, lon_cols)
    window_labels = to_windows(labels[..., None])[..., 0]

    def window_block(grid_cells, table_values):
        block_rows = attend(
            to_windows(grid_cells), window_labels, table_values, bias_index, qkv_weight, proj_weight
        )
        return from_windows(block_rows, level_count, lat_rows, lon_cols)

    rolled = roll_forward(latents)
    rolled_out, block_pull = jax.vjp(window_block, rolled, bias_table)
    restored = roll_back(rolled_out)
    merge_in, norm_pull = jax.vjp(merge_inputs, restored)
    token_rows = merge_in.shape[0]
    cotangent_rows = cotangent.reshape(token_rows, out_width)
    weight_piece = lax.all_gather(merge_weight, "lon", axis=0, tiled=True)
    running = jnp.dot(merge_in, weight_piece, preferred_element_type=jnp.float32)
    grad_columns = lax.dot_general(
        cotangent_rows, weight_piece, (((1,), (1,)), ((), ())), preferred_element_type=jnp.float32
    ).astype(jnp.bfloat16)
    running, merge_grad = (running, grad_columns)
    merged_rows = running.astype(jnp.bfloat16)
    merged = merged_rows.reshape(level_count, lat_rows // 2, lon_cols // 2, out_width)
    restored_grad = norm_pull(merge_grad)[0]
    rolled_grad = roll_forward(restored_grad)
    grad_rolled, grad_table = block_pull(rolled_grad)
    grad_latents = roll_back(grad_rolled)
    grad_bias = lax.psum(grad_table, ("lon", "lat"))
    return (merged, grad_latents, grad_bias)


def solution(mesh):
    return jax.shard_map(
        shards,
        mesh=mesh,
        in_specs=(
            P(None, "lat", "lon", None),
            P(),
            P(),
            P("lon", None),
            P(),
            P(),
            P(None, "lat", "lon", None),
        ),
        out_specs=(P(None, "lat", "lon", None), P(None, "lat", "lon", None), P()),
        check_vma=False,
    )
```

profile of v0, /device:TPU:1, one launch (start us, length us, event | category | flops | bytes accessed | tf_op | source)
XLA Modules:
  0.0 500.5 jit_solution(5109473167508686739)
XLA Ops:
  7.9 1.3 slice.92
  9.2 1.4 slice.91
  10.6 1.3 fusion.49
  12.0 6.0 %collective-permute-start = (bf16[4,6,6,1024]{3,0,2,1:T(4,128)(2,1)}, bf16[4,6,6,1024]{3,0,2,1:T(4,128)(2,1)S(1)}, u32[]{:S(2)}, u32[]{:S(2)}) collective-permute-start(bf16[4,6,6,1024]{3,0,2,1:T(4,128)(2,1)} %get-tuple-element.26), channel_id=1, source_target_pairs={{0,7},{1,0},{2,1},{3,2},{4,3},{5,4},{6,5},{7,6},{8,15},{9,8},{10,9... | collective-permute-start | bytes 884744 | tf_op jit(solution)/shard_map/ppermute | solution.py:17
  19.1 38.9 %gather_fusion = f32[20736,16]{1,0:T(8,128)} fusion(f32[16,759]{0,1:T(8,128)S(1)} %copy.88, s32[21504]{0:T(1024)S(1)} %pad_clamp_fusion), kind=kCustom, calls=%fused_computation | custom fusion | bytes 2737152 | tf_op jit(solution)/shard_map/jvp(jit(_take))/gather | solution.py:85
  58.0 12.2 %copy.89 = f32[144,144,16]{0,1,2:T(8,128)} copy(f32[144,144,16]{2,1,0:T(8,128)} %bitcast.68) | data formatting | bytes 2654208 | tf_op jit(solution)/shard_map/jvp(jit(_take))/gather | solution.py:85
  71.8 3.4 select_bitcast_fusion
  75.2 8.5 %collective-permute-done.1 = bf16[4,12,3,1024]{3,0,2,1:T(4,128)(2,1)S(1)} collective-permute-done((bf16[4,12,3,1024]{3,0,2,1:T(4,128)(2,1)S(1)}, bf16[4,12,3,1024]{3,0,2,1:T(4,128)(2,1)S(1)}, u32[]{:S(2)}, u32[]{:S(2)}) %collective-permute-start.1) | collective-permute-done | bytes 294944 | tf_op jit(solution)/shard_map/ppermute | solution.py:17
  85.6 1.9 copy.81
  87.5 1.7 reshape.228
  89.3 6.6 %convolution_convert_fusion.1 = bf16[288,3072]{1,0:T(8,128)(2,1)} fusion(bf16[1024,3072]{1,0:T(8,128)(2,1)} %param.8, f32[288,1024]{1,0:T(8,128)S(1)} %reshape.228, f32[288]{0:T(512)S(1)} %rsqrt.20, f32[288]{0:T(512)S(1)} %div.66), kind=kOutput, calls=%fused_computation.19 | convolution fusion | flops 1813708800 | bytes 9242880 | tf_op jit(solution)/shard_map/jvp()/dot_general | solution.py:80
  95.9 5.7 %reshape.218 = bf16[2,144,3,16,64]{4,3,2,1,0:T(8,128)(2,1)} reshape(bf16[288,3072]{1,0:T(8,128)(2,1)} %convolution_convert_fusion.1) | data formatting | bytes 3538944 | tf_op jit(solution)/shard_map/jvp()/reshape | solution.py:81
  101.6 4.1 fusion.64
  105.7 2.8 copy.116
  108.5 2.9 copy.117
  111.4 2.8 copy.118
  114.2 3.9 fusion.10
  118.1 1.4 fusion.59
  120.2 4.1 convert_reduce_fusion
  124.3 1.4 copy-done.5
  125.7 1.5 fusion.20
  127.3 2.9 copy.91
  130.2 2.7 reshape.219
  132.9 2.7 fusion.28
  135.5 1.3 reshape.220
  137.7 4.7 collective-permute-done.2
  144.6 11.0 %collective-permute-done.3 = bf16[4,6,6,1024]{3,2,1,0:T(8,128)(2,1)} collective-permute-done((bf16[4,6,6,1024]{3,2,1,0:T(8,128)(2,1)}, bf16[4,6,6,1024]{3,2,1,0:T(8,128)(2,1)}, u32[]{:S(2)}, u32[]{:S(2)}) %collective-permute-start.3) | collective-permute-done | bytes 294944 | tf_op jit(solution)/shard_map/ppermute | solution.py:17
  155.6 1.3 fusion.39
  157.7 2.0 copy.93
  159.9 2.3 reshape.229
  162.4 1.7 multiply_reduce_fusion.1
  164.5 12.2 %multiply_reduce_fusion = (f32[72]{0:T(128)S(1)}, f32[72,4096]{1,0:T(8,128)}) fusion(f32[72,4096]{1,0:T(8,128)S(1)} %reshape.229, f32[72]{0:T(128)S(1)} %div.71, bf16[72,2048]{1,0:T(8,128)(2,1)} %reshape.222, bf16[4096,2048]{1,0:T(8,128)(2,1)} %all-gather.2.cloned.1.call-done), kind=kOutput, calls=%fused_computation.48 | convolution fusion | flops 1209433984 | bytes 19432000 | tf_op jit(solution)/shard_map/dot_general | solution.py:153
  176.8 1.7 fusion.63
  179.4 2.8 reshape.223
  183.3 1.3 slice.133
  187.5 2.0 slice.107
  191.0 8.9 %collective-permute-done.4 = bf16[4,6,6,1024]{3,2,1,0:T(8,128)(2,1)S(1)} collective-permute-done((bf16[4,6,6,1024]{3,2,1,0:T(8,128)(2,1)S(1)}, bf16[4,6,6,1024]{3,2,1,0:T(8,128)(2,1)S(1)}, u32[]{:S(2)}, u32[]{:S(2)}) %collective-permute-start.4) | collective-permute-done | bytes 294944 | tf_op jit(solution)/shard_map/ppermute | solution.py:17
  200.2 4.2 collective-permute-start.5
  204.4 8.2 %collective-permute-done.5 = bf16[4,12,3,1024]{3,2,1,0:T(4,128)(2,1)S(1)} collective-permute-done((bf16[4,12,3,1024]{3,2,1,0:T(4,128)(2,1)S(1)}, bf16[4,12,3,1024]{3,2,1,0:T(4,128)(2,1)S(1)}, u32[]{:S(2)}, u32[]{:S(2)}) %collective-permute-start.5) | collective-permute-done | bytes 294944 | tf_op jit(solution)/shard_map/ppermute | solution.py:17
  212.6 1.3 pad_maximum_fusion.8
  213.8 2.1 reshape.224
  215.9 2.7 convolution_convert_fusion.7
  218.6 1.9 reshape.225
  220.4 1.9 copy.99
  222.4 3.0 fusion.21
  225.4 5.8 %fusion.3 = (f32[2,16,144]{2,1,0:T(8,128)S(1)}, bf16[2,16,144,144]{2,3,1,0:T(8,128)(2,1)S(1)}) fusion(f32[2,16,144]{2,1,0:T(8,128)S(1)} %multiply_divide_fusion, f32[2,16,144]{2,1,0:T(8,128)S(1)} %copy-done.20, f32[16,144,144]{1,2,0:T(8,128)} %select_bitcast_fusion, f32[2,16,144,144]{2,3,1,0:T(8,128)} %copy-done.2, ...), kind=kOutput, calls=%fused_computation.7 | convolution fusion | flops 90902016 | bytes 6584832 | tf_op jit(solution)/shard_map/transpose(jvp(whqk,wkhd->wqhd))/dot_general | solution.py:91
  231.4 2.5 fusion.60
  233.9 1.3 fusion.22
  236.0 1.5 fusion.25
  237.4 2.5 pad_add_fusion
  239.9 6.6 %copy.104 = bf16[2,144,3,16,64]{4,3,2,1,0:T(8,128)(2,1)} copy(bf16[2,144,3,16,64]{1,4,3,0,2:T(8,128)(2,1)} %pad_add_fusion) | data formatting | bytes 3538944 | tf_op jit(solution)/shard_map/transpose(jvp())/add_any | solution.py:83
  246.6 6.0 %reshape.226 = bf16[288,3072]{1,0:T(8,128)(2,1)} reshape(bf16[2,144,3,16,64]{4,3,2,1,0:T(8,128)(2,1)} %copy.104) | data formatting | bytes 3538944 | tf_op jit(solution)/shard_map/transpose(jvp())/reshape | solution.py:81
  252.6 5.5 %fusion.29 = (f32[288]{0:T(512)S(1)}, bf16[288,1024]{1,0:T(8,128)(2,1)S(1)}) fusion(f32[288,1024]{1,0:T(8,128)S(1)} %copy-done.9, f32[288]{0:T(512)S(1)} %div.66, bf16[288,3072]{1,0:T(8,128)(2,1)} %reshape.226, bf16[1024,3072]{1,0:T(8,128)(2,1)} %param.8), kind=kOutput, calls=%fused_computation.45 | convolution fusion | flops 1813413632 | bytes 9832704 | tf_op jit(solution)/shard_map/transpose(jvp())/dot_general | solution.py:80
  259.1 1.3 fusion.40
  260.4 1.3 reshape.227
  262.7 9.7 %convolution_convert_fusion.2 = bf16[72,2048]{1,0:T(8,128)(2,1)} fusion(bf16[4096,2048]{1,0:T(8,128)(2,1)} %all-gather.2.cloned.1.call-done, f32[72,4096]{1,0:T(8,128)S(1)} %reshape.229, f32[72]{0:T(128)S(1)} %copy-done.33, f32[72]{0:T(128)S(1)} %copy-done.31), kind=kOutput, calls=%fused_computation.26 | convolution fusion | flops 1208991744 | bytes 18252352 | tf_op jit(solution)/shard_map/dot_general | solution.py:152
  272.5 1.2 reshape.221
  274.7 1.9 fusion.45
  276.6 5.2 %fusion.13 = f32[16,144,144]{1,2,0:T(8,128)} fusion(f32[2,16,144,144]{2,3,1,0:T(8,128)} %copy-done.6, pred[2,16,144,144]{2,3,1,0:T(8,128)(4,1)S(1)} %copy-done.11, f32[2,16,144]{2,1,0:T(8,128)S(1)} %negate_divide_fusion, pred[2,144,144]{1,2,0:T(8,128)(4,1)S(1)} %broadcast_compare_fusion), kind=kLoop, calls=%fused_computation.30 | loop fusion | flops 2322432 | bytes 4704768 | tf_op jit(solution)/shard_map/transpose(jvp())/reduce_sum | solution.py:87
  281.9 11.0 %copy.114 = f32[144,144,16]{2,1,0:T(8,128)} copy(f32[144,144,16]{0,1,2:T(8,128)} %bitcast.70) | data formatting | bytes 2654208 | tf_op jit(solution)/shard_map/transpose(jvp())/reduce_sum | solution.py:87
  292.9 112.6 %scatter_custom_fusion = f32[16,759]{0,1:T(8,128)S(1)} fusion(s32[20736]{0:T(1024)} %copy-done.24, f32[20736,16]{1,0:T(8,128)} %bitcast.69, f32[]{:T(128)} %constant.21.clone.1), kind=kCustom, calls=%fused_computation.97 | custom fusion | flops 331776 | bytes 49088 | tf_op jit(solution)/shard_map/transpose(jvp(jit(_take)))/scatter-add | solution.py:85
  405.5 84.3 %psum.7 = f32[16,759]{0,1:T(8,128)S(1)} all-reduce(f32[16,759]{0,1:T(8,128)S(1)} %scatter_custom_fusion), channel_id=1, replica_groups=mesh['lon'=32,'lat'=8] {'lon','lat'}, use_global_device_ids=true, to_apply=%region_15.16 | all-reduce | flops 12144 | bytes 97152 | tf_op jit(solution)/shard_map/psum | solution.py:163
  490.6 1.3 fusion.37
  491.9 1.3 copy.108
  (139 shorter events, 21.8 us)
Async XLA Ops:
  7.2 125.7 %copy-start = (bf16[1024,1024]{1,0:T(8,128)(2,1)S(1)}, bf16[1024,1024]{1,0:T(8,128)(2,1)}, u32[]{:S(2)}) copy-start(bf16[1024,1024]{1,0:T(8,128)(2,1)} %param.9) | copy-start | bytes 6291460
  7.2 10.8 %copy-start.18 = (s32[144,144]{1,0:T(8,128)S(1)}, s32[144,144]{1,0:T(8,128)}, u32[]{:S(2)}) copy-start(s32[144,144]{1,0:T(8,128)} %param.12) | copy-start | bytes 248836
  7.2 157.3 %all-gather.2.cloned.1.call-start = ((), (), s32[]{:S(2)}) async-start(), calls=%async_computation | async-start | bytes 17301504 | tf_op jit(solution)/shard_map/all_gather | solution.py:151
  7.9 11.0 %copy-start.27 = (f32[16,759]{1,0:T(8,128)S(1)}, f32[16,759]{1,0:T(8,128)}, u32[]{:S(2)}) copy-start(f32[16,759]{1,0:T(8,128)} %param.11) | copy-start | bytes 145732
  12.0 58.3 %collective-permute-start = (bf16[4,6,6,1024]{3,0,2,1:T(4,128)(2,1)}, bf16[4,6,6,1024]{3,0,2,1:T(4,128)(2,1)S(1)}, u32[]{:S(2)}, u32[]{:S(2)}) collective-permute-start(bf16[4,6,6,1024]{3,0,2,1:T(4,128)(2,1)} %get-tuple-element.26), channel_id=1, source_target_pairs={{0,7},{1,0},{2,1},{3,2},{4,3},{5,4},{6,5},{7,6},{8,15},{9,8},{10,9... | collective-permute-start | bytes 884744 | tf_op jit(solution)/shard_map/ppermute | solution.py:17
  18.2 0.6 copy-start.24
  70.7 12.9 %collective-permute-start.1 = (bf16[4,12,3,1024]{3,0,2,1:T(4,128)(2,1)S(1)}, bf16[4,12,3,1024]{3,0,2,1:T(4,128)(2,1)S(1)}, u32[]{:S(2)}, u32[]{:S(2)}) collective-permute-start(bf16[4,12,3,1024]{3,0,2,1:T(4,128)(2,1)S(1)} %get-tuple-element.36), channel_id=1, source_target_pairs={{0,248},{8,0},{16,8},{24,16},{32,24},{40,32},{48,40},{56,48},{64,5... | collective-permute-start | bytes 884744 | tf_op jit(solution)/shard_map/ppermute | solution.py:17
  85.2 4.0 copy-start.28
  89.3 43.6 %copy-start.8 = (f32[288,1024]{1,0:T(8,128)}, f32[288,1024]{1,0:T(8,128)S(1)}, u32[]{:S(2)}) copy-start(f32[288,1024]{1,0:T(8,128)S(1)} %reshape.228) | copy-start | bytes 3538948
  114.2 3.9 copy-start.3
  118.1 2.1 copy-start.2
  118.1 2.1 copy-start.19
  120.2 4.1 copy-start.21
  120.2 5.5 %copy-start.12 = (bf16[2,144,1,16,64]{1,4,3,0,2:T(8,128)(2,1)S(1)}, bf16[2,144,1,16,64]{1,4,3,0,2:T(8,128)(2,1)}, u32[]{:S(2)}) copy-start(bf16[2,144,1,16,64]{1,4,3,0,2:T(8,128)(2,1)} %copy.116) | copy-start | bytes 1769476
  124.3 1.4 copy-start.5
  136.8 6.5 %copy-start.25 = (bf16[4,6,3,2048]{3,0,2,1:T(4,128)(2,1)S(1)}, bf16[4,6,3,2048]{3,0,2,1:T(4,128)(2,1)}, u32[]{:S(2)}) copy-start(bf16[4,6,3,2048]{3,0,2,1:T(4,128)(2,1)} %param.13) | copy-start | bytes 884740
  137.1 5.3 %collective-permute-start.2 = (bf16[4,12,3,1024]{3,2,1,0:T(4,128)(2,1)S(1)}, bf16[4,12,3,1024]{3,2,1,0:T(4,128)(2,1)S(1)}, u32[]{:S(2)}, u32[]{:S(2)}) collective-permute-start(bf16[4,12,3,1024]{3,2,1,0:T(4,128)(2,1)S(1)} %get-tuple-element.34), channel_id=1, source_target_pairs={{0,8},{8,16},{16,24},{24,32},{32,40},{40,48},{48,56},{56,64},{64,7... | collective-permute-start | bytes 884744 | tf_op jit(solution)/shard_map/ppermute | solution.py:17
  143.3 12.2 %collective-permute-start.3 = (bf16[4,6,6,1024]{3,2,1,0:T(8,128)(2,1)}, bf16[4,6,6,1024]{3,2,1,0:T(8,128)(2,1)}, u32[]{:S(2)}, u32[]{:S(2)}) collective-permute-start(bf16[4,6,6,1024]{3,2,1,0:T(8,128)(2,1)} %fusion.47), channel_id=1, source_target_pairs={{0,1},{1,2},{2,3},{3,4},{4,5},{5,6},{6,7},{7,0},{8,9},{9,10},{10,1... | collective-permute-start | bytes 884744 | tf_op jit(solution)/shard_map/ppermute | solution.py:17
  157.6 2.0 copy-start.7
  164.4 12.3 %copy-start.30 = (f32[72]{0:T(128)}, f32[72]{0:T(128)S(1)}, u32[]{:S(2)}) copy-start(f32[72]{0:T(128)S(1)} %div.71) | copy-start | bytes 868
  176.7 2.7 copy-start.32
  189.5 14.9 %copy-start.22 = (f32[2,16,144]{2,1,0:T(8,128)S(1)}, f32[2,16,144]{2,1,0:T(8,128)}, u32[]{:S(2)}) copy-start(f32[2,16,144]{2,1,0:T(8,128)} %copy-done.21) | copy-start | bytes 55300
  190.7 9.1 %collective-permute-start.4 = (bf16[4,6,6,1024]{3,2,1,0:T(8,128)(2,1)S(1)}, bf16[4,6,6,1024]{3,2,1,0:T(8,128)(2,1)S(1)}, u32[]{:S(2)}, u32[]{:S(2)}) collective-permute-start(bf16[4,6,6,1024]{3,2,1,0:T(8,128)(2,1)S(1)} %get-tuple-element.32), channel_id=1, source_target_pairs={{0,7},{1,0},{2,1},{3,2},{4,3},{5,4},{6,5},{7,6},{8,15},{9,8},{10,9... | collective-permute-start | bytes 884744 | tf_op jit(solution)/shard_map/ppermute | solution.py:17
  200.2 12.4 %collective-permute-start.5 = (bf16[4,12,3,1024]{3,2,1,0:T(4,128)(2,1)S(1)}, bf16[4,12,3,1024]{3,2,1,0:T(4,128)(2,1)S(1)}, u32[]{:S(2)}, u32[]{:S(2)}) collective-permute-start(bf16[4,12,3,1024]{3,2,1,0:T(4,128)(2,1)S(1)} %get-tuple-element.30), channel_id=1, source_target_pairs={{0,248},{8,0},{16,8},{24,16},{32,24},{40,32},{48,40},{56,48},{64,5... | collective-permute-start | bytes 884744 | tf_op jit(solution)/shard_map/ppermute | solution.py:17
  222.4 3.0 copy-start.20
  222.4 8.9 %slice-start = ((s8[4718592]{0:T(1024)(128)(4,1)}), s8[4194304]{0:T(1024)(128)(4,1)S(1)}, s32[]{:S(2)}) async-start(s8[4718592]{0:T(1024)(128)(4,1)} %bitcast.63), calls=%async_computation.1 | async-start | bytes 8388608
  225.4 5.9 %slice-start.1 = ((s8[4718592]{0:T(1024)(128)(4,1)}), s8[524288]{0:T(1024)(128)(4,1)S(1)}, s32[]{:S(2)}) async-start(s8[4718592]{0:T(1024)(128)(4,1)} %bitcast.63), calls=%async_computation.2 | async-start | bytes 1048576
  225.4 5.9 %copy-start.4 = (f32[16,144,144]{1,2,0:T(8,128)S(1)}, f32[16,144,144]{1,2,0:T(8,128)}, u32[]{:S(2)}) copy-start(f32[16,144,144]{1,2,0:T(8,128)} %select_bitcast_fusion) | copy-start | bytes 3981316
  225.4 5.9 %copy-start.23 = (f32[2,16,144]{2,1,0:T(8,128)S(1)}, f32[2,16,144]{2,1,0:T(8,128)}, u32[]{:S(2)}) copy-start(f32[2,16,144]{2,1,0:T(8,128)} %copy-done.21) | copy-start | bytes 55300
  231.3 2.5 copy-start.26
  231.3 2.5 copy-start.10
  231.4 2.5 copy-start.14
  233.8 2.1 copy-start.6
  233.9 2.1 copy-start.13
  246.6 6.0 %copy-start.9 = (f32[288,1024]{1,0:T(8,128)S(1)}, f32[288,1024]{1,0:T(8,128)}, u32[]{:S(2)}) copy-start(f32[288,1024]{1,0:T(8,128)} %copy-done.8) | copy-start | bytes 3538948
  252.6 5.5 %copy-start.29 = (f32[288]{0:T(512)S(1)}, f32[288]{0:T(512)}, u32[]{:S(2)}) copy-start(f32[288]{0:T(512)} %copy-done.28) | copy-start | bytes 3460
  258.1 1.1 copy-start.17
  260.4 2.3 copy-start.31
  260.4 2.3 copy-start.33
  262.7 12.0 %copy-start.15 = (bf16[4,12,3,1024]{3,2,1,0:T(4,128)(2,1)}, bf16[4,12,3,1024]{3,2,1,0:T(4,128)(2,1)S(1)}, u32[]{:S(2)}) copy-start(bf16[4,12,3,1024]{3,2,1,0:T(4,128)(2,1)S(1)} %get-tuple-element.27) | copy-start | bytes 884740
  262.7 12.0 %collective-permute-start.6 = (bf16[4,12,3,1024]{3,2,1,0:T(4,128)(2,1)}, bf16[4,12,3,1024]{3,2,1,0:T(4,128)(2,1)}, u32[]{:S(2)}, u32[]{:S(2)}) collective-permute-start(bf16[4,12,3,1024]{3,2,1,0:T(4,128)(2,1)} %get-tuple-element.28), channel_id=1, source_target_pairs={{0,8},{8,16},{16,24},{24,32},{32,40},{40,48},{48,56},{56,64},{64,7... | collective-permute-start | bytes 884744 | tf_op jit(solution)/shard_map/ppermute | solution.py:17
  272.5 4.1 copy-start.11
  276.6 214.0 %collective-permute-start.7 = (bf16[4,6,6,1024]{3,2,1,0:T(8,128)(2,1)}, bf16[4,6,6,1024]{3,2,1,0:T(8,128)(2,1)}, u32[]{:S(2)}, u32[]{:S(2)}) collective-permute-start(bf16[4,6,6,1024]{3,2,1,0:T(8,128)(2,1)} %fusion.45), channel_id=1, source_target_pairs={{0,1},{1,2},{2,3},{3,4},{4,5},{5,6},{6,7},{7,0},{8,9},{9,10},{10,1... | collective-permute-start | bytes 884744 | tf_op jit(solution)/shard_map/ppermute | solution.py:17
  281.8 208.7 %copy-start.16 = (bf16[4,12,3,1024]{3,2,1,0:T(4,128)(2,1)S(1)}, bf16[4,12,3,1024]{3,2,1,0:T(4,128)(2,1)}, u32[]{:S(2)}) copy-start(bf16[4,12,3,1024]{3,2,1,0:T(4,128)(2,1)} %copy-done.15) | copy-start | bytes 884740
  292.9 200.3 %copy-start.1 = (bf16[1024,1024]{1,0:T(8,128)(2,1)S(1)}, bf16[1024,1024]{1,0:T(8,128)(2,1)}, u32[]{:S(2)}) copy-start(bf16[1024,1024]{1,0:T(8,128)(2,1)} %param.9) | copy-start | bytes 6291460
Sparse Core Ops, SparseCore 0:
  9.9 107.1 all-gather.1
where the time goes:
time: 508 us; the launch traced here: 500 us
  other arithmetic  148 us (29%)
  local copies, waits for them, and re-layouts  142 us (28%)
  blocking collectives  84.3 us (17%)
  matrix products  56.5 us (11%)
  waiting for transfers between devices  41.9 us (8%)
  between operations  15.2 us (3%)
  starting transfers between devices  12.1 us (2%)
    scatter-add x1, other arithmetic, attend(): bias_terms = jnp.take(bias_table, bias_index, axis=1)  113 us
    psum x1, blocking collectives, shards(): grad_bias = lax.psum(grad_table, ('lon', 'lat'))  84.3 us
    gather x2, local copies, waits for them, and re-layouts, attend(): bias_terms = jnp.take(bias_table, bias_index, axis=1)  51.1 us
    ppermute x8, waiting for transfers between devices, from_behind(): lax.ppermute(shard, axis, [(i, (i + by) % devices) for i in range(devices)])  41.2 us
    unnamed x81, local copies, waits for them, and re-layouts  16.9 us
    dot_general x1, matrix products, shards(): lax.dot_general(cotangent_rows, weight_piece, (((1,), (1,)), ((), ())), p...  12.2 us
    dot_general x2, matrix products, attend(): jnp.dot(normed, qkv_weight, preferred_element_type=jnp.float32)  12.1 us
    ppermute x8, starting transfers between devices, from_behind(): lax.ppermute(shard, axis, [(i, (i + by) % devices) for i in range(devices)])  12.1 us
  transfers between devices with their start and end apart: 9, of which 5 were waited for; matrix products, arithmetic and copies ran while one was open for 53% of the time, Pallas kernels for 0%

commit v1 on v0

v1 whole, which is shorter than its diff:
```python
import jax
import jax.numpy as jnp
from jax import lax
from jax.experimental import pallas as pl
from jax.experimental.pallas import tpu as pltpu
from jax.sharding import PartitionSpec as P

EPS = 1e-05
MASKED = -1e30
HEADS = 16
PAIRS = 8
HEAD_DIM = 64
WINDOW = 144
WINDOWS = 2
TOKENS = WINDOW * WINDOWS
WIDTH = 1024
BUCKETS = 768
LANES = 128
SPLIT = 256
WIN_LEV = 2
WIN_LAT = 12
WIN_LON = 6
F32 = jnp.float32
BF16 = jnp.bfloat16
LAST = (((1,), (1,)), ((), ()))
FIRST = (((0,), (0,)), ((), ()))


def dot(a, b, dims=(((1,), (0,)), ((), ()))):
    return lax.dot_general(a, b, dims, preferred_element_type=F32)


def stats(values):
    average = jnp.mean(values, axis=-1, keepdims=True)
    centered = values - average
    variance = jnp.mean(centered * centered, axis=-1, keepdims=True)
    return centered, lax.rsqrt(variance + EPS)


def half_mask(shape, half):
    lane = lax.broadcasted_iota(jnp.int32, shape, 1)
    return (lane >= HEAD_DIM) if half else (lane < HEAD_DIM)


def region_code(shape, axis, window, is_last):
    token = lax.broadcasted_iota(jnp.int32, shape, axis)
    level = (token >= 72).astype(jnp.int32)
    row = token - 72 * level
    late = (row >= 36).astype(jnp.int32)
    return late * is_last + (2 * level if window == 1 else 0)


def allowed_pairs(window, is_last):
    shape = (WINDOW, WINDOW)
    return region_code(shape, 0, window, is_last) == region_code(shape, 1, window, is_last)


def gather_bias(table_ref, index_ref, head):
    tiles = []
    for tile in range(2):
        index = index_ref[:, tile * LANES:(tile + 1) * LANES]
        low = index & (LANES - 1)
        high = index >> 7
        found = None
        for chunk in range(BUCKETS // LANES):
            row = table_ref[head:head + 1, chunk * LANES:(chunk + 1) * LANES]
            spread = jnp.broadcast_to(row, (WINDOW, LANES))
            part = jnp.take_along_axis(spread, low, axis=1, mode="promise_in_bounds")
            found = part if found is None else jnp.where(high == chunk, part, found)
        tiles.append(found)
    return jnp.concatenate(tiles, axis=1)[:, :WINDOW]


def forward_body(is_last, x_ref, table_ref, index_ref, wqkv_ref, wproj_ref, out_ref, packed_ref, probs_ref, normed, attended):
    centered, inverse = stats(x_ref[...].astype(F32))
    normed[...] = (centered * inverse).astype(BF16)
    for part in range(12):
        cols = slice(part * 256, (part + 1) * 256)
        packed_ref[:, cols] = dot(normed[...], wqkv_ref[:, cols]).astype(BF16)
    allowed = [allowed_pairs(window, is_last) for window in range(WINDOWS)]
    for pair in range(PAIRS):
        bias = [gather_bias(table_ref, index_ref, 2 * pair + half) for half in range(2)]
        for window in range(WINDOWS):
            rows = slice(window * WINDOW, (window + 1) * WINDOW)
            base = pair * LANES
            query = packed_ref[rows, base:base + LANES] * jnp.array(HEAD_DIM ** -0.5, BF16)
            key = packed_ref[rows, WIDTH + base:WIDTH + base + LANES]
            value = packed_ref[rows, 2 * WIDTH + base:2 * WIDTH + base + LANES]
            masks = [half_mask((WINDOW, LANES), half) for half in range(2)]
            zero = jnp.zeros((WINDOW, LANES), BF16)
            mixed = None
            for half in range(2):
                scores = dot(jnp.where(masks[half], query, zero), key, LAST)
                scores = jnp.where(allowed[window], scores + bias[half], MASKED)
                weights = jnp.exp(scores - jnp.max(scores, axis=-1, keepdims=True))
                probs = (weights * (1.0 / jnp.sum(weights, axis=-1, keepdims=True))).astype(BF16)
                probs_ref[window, 2 * pair + half] = probs
                term = dot(probs, jnp.where(masks[half], value, zero))
                mixed = term if mixed is None else mixed + term
            attended[rows, base:base + LANES] = mixed.astype(BF16)
    for part in range(4):
        cols = slice(part * 256, (part + 1) * 256)
        out_ref[:, cols] = (x_ref[:, cols].astype(F32) + dot(attended[...], wproj_ref[:, cols])).astype(BF16)


def forward_kernel(x_ref, table_ref, index_ref, wqkv_ref, wproj_ref, out_ref, packed_ref, probs_ref, normed, attended):
    is_last = (lax.axis_index("lat") == lax.axis_size("lat") - 1).astype(jnp.int32)
    forward_body(is_last, x_ref, table_ref, index_ref, wqkv_ref, wproj_ref, out_ref, packed_ref, probs_ref, normed, attended)


def forward_call(x, table, index, wqkv, wproj, kernel=forward_kernel):
    return pl.pallas_call(
        kernel,
        out_shape=(
            jax.ShapeDtypeStruct((TOKENS, WIDTH), BF16),
            jax.ShapeDtypeStruct((TOKENS, 3 * WIDTH), BF16),
            jax.ShapeDtypeStruct((WINDOWS, HEADS, WINDOW, WINDOW), BF16),
        ),
        in_specs=[pl.BlockSpec(memory_space=pltpu.VMEM)] * 5,
        out_specs=[pl.BlockSpec(memory_space=pltpu.VMEM)] * 3,
        scratch_shapes=[pltpu.VMEM((TOKENS, WIDTH), BF16), pltpu.VMEM((TOKENS, WIDTH), BF16)],
        compiler_params=pltpu.CompilerParams(vmem_limit_bytes=56 * 2**20),
        cost_estimate=pl.CostEstimate(flops=2 * 1400 * 2**20, bytes_accessed=16 * 2**20, transcendentals=0),
        name="attention_forward",
    )(x, table, index, wqkv, wproj)


def backward_kernel(grad_ref, x_ref, packed_ref, probs_ref, index_ref, wqkv_ref, wproj_ref, dx_ref, table_ref, datt, dpacked, dmain, dtail):
    datt[...] = dot(grad_ref[...], wproj_ref[...], LAST).astype(BF16)
    for pair in range(PAIRS):
        sums = [None, None]
        for window in range(WINDOWS):
            rows = slice(window * WINDOW, (window + 1) * WINDOW)
            base = pair * LANES
            scale = jnp.array(HEAD_DIM ** -0.5, BF16)
            query = packed_ref[rows, base:base + LANES] * scale
            key = packed_ref[rows, WIDTH + base:WIDTH + base + LANES] * scale
            value = packed_ref[rows, 2 * WIDTH + base:2 * WIDTH + base + LANES]
            out_grad = datt[rows, base:base + LANES]
            masks = [half_mask((WINDOW, LANES), half) for half in range(2)]
            zero = jnp.zeros((WINDOW, LANES), BF16)
            dquery, dkey, dvalue = None, None, None
            for half in range(2):
                grad = jnp.where(masks[half], out_grad, zero)
                probs = probs_ref[window, 2 * pair + half]
                wide = probs.astype(F32)
                dprobs = dot(grad, value, LAST)
                product = wide * dprobs
                ds = product - wide * jnp.sum(product, axis=-1, keepdims=True)
                sums[half] = ds if sums[half] is None else sums[half] + ds
                narrow = ds.astype(BF16)
                one = dot(narrow, jnp.where(masks[half], key, zero))
                two = dot(narrow, jnp.where(masks[half], query, zero), FIRST)
                three = dot(probs, grad, FIRST)
                dquery = one if dquery is None else dquery + one
                dkey = two if dkey is None else dkey + two
                dvalue = three if dvalue is None else dvalue + three
            dpacked[rows, base:base + LANES] = dquery.astype(BF16)
            dpacked[rows, WIDTH + base:WIDTH + base + LANES] = dkey.astype(BF16)
            dpacked[rows, 2 * WIDTH + base:2 * WIDTH + base + LANES] = dvalue.astype(BF16)
        for half in range(2):
            total = jnp.concatenate([sums[half], jnp.zeros((WINDOW, 2 * LANES - WINDOW), F32)], axis=1)
            for tile in range(2):
                cols = slice(tile * LANES, (tile + 1) * LANES)
                dscores = (dmain, dtail)[tile]
                dscores[pl.ds(2 * pair + half, WINDOW, stride=HEADS), :] = total[:, cols]
    dnormed = dot(dpacked[...], wqkv_ref[...], LAST).astype(BF16).astype(F32)
    centered, inverse = stats(x_ref[...].astype(F32))
    hat = centered * inverse
    slope = jnp.mean(dnormed * hat, axis=-1, keepdims=True)
    inner = inverse * (dnormed - jnp.mean(dnormed, axis=-1, keepdims=True) - hat * slope)
    dx_ref[...] = (grad_ref[...].astype(F32) + inner).astype(BF16)

    def scatter_row(row, total):
        here = pl.ds(pl.multiple_of(row * HEADS, HEADS), HEADS)
        block = jnp.concatenate([dmain[here, :], dtail[here, :]], axis=1)
        index = index_ref[pl.ds(row, 1), :]
        low = index & (SPLIT - 1)
        high = index >> 8
        parts = jnp.concatenate(
            [jnp.where(high == part, block, 0.0) for part in range(BUCKETS // SPLIT)], axis=0
        )
        coarse = parts.astype(BF16)
        fine = (parts - coarse.astype(F32)).astype(BF16)
        bucket = lax.broadcasted_iota(jnp.int32, (SPLIT, 2 * LANES), 0)
        hot = jnp.where(bucket == low, 1.0, 0.0).astype(BF16)
        return total + dot(jnp.concatenate([coarse, fine], axis=0), hot, LAST)

    rows = HEADS * (BUCKETS // SPLIT)
    total = lax.fori_loop(0, WINDOW, scatter_row, jnp.zeros((2 * rows, SPLIT), F32), unroll=4)
    total = total[:rows] + total[rows:]
    for part in range(BUCKETS // SPLIT):
        table_ref[:, part * SPLIT:(part + 1) * SPLIT] = total[part * HEADS:(part + 1) * HEADS]


def backward_call(grad, x, packed, probs, index, wqkv, wproj):
    return pl.pallas_call(
        backward_kernel,
        out_shape=(
            jax.ShapeDtypeStruct((TOKENS, WIDTH), BF16),
            jax.ShapeDtypeStruct((HEADS, BUCKETS), F32),
        ),
        in_specs=[pl.BlockSpec(memory_space=pltpu.VMEM)] * 7,
        out_specs=[pl.BlockSpec(memory_space=pltpu.VMEM)] * 2,
        scratch_shapes=[
            pltpu.VMEM((TOKENS, WIDTH), BF16),
            pltpu.VMEM((TOKENS, 3 * WIDTH), BF16),
            pltpu.VMEM((WINDOW * HEADS, LANES), F32),
            pltpu.VMEM((WINDOW * HEADS, LANES), F32),
        ],
        compiler_params=pltpu.CompilerParams(vmem_limit_bytes=56 * 2**20),
        cost_estimate=pl.CostEstimate(flops=2 * 1700 * 2**20, bytes_accessed=16 * 2**20, transcendentals=0),
        name="attention_backward",
    )(grad, x, packed, probs, index, wqkv, wproj)


def from_behind(shard, axis, by):
    devices = lax.axis_size(axis)
    return lax.ppermute(shard, axis, [(i, (i + by) % devices) for i in range(devices)])


def normalize(values):
    average = jnp.mean(values, axis=-1, keepdims=True)
    centered = values - average
    variance = jnp.mean(centered * centered, axis=-1, keepdims=True)
    return centered * lax.rsqrt(variance + EPS)


def to_windows(grid_cells):
    level_count, lat_rows, lon_cols, features = grid_cells.shape
    shaped = grid_cells.reshape(
        level_count // WIN_LEV,
        WIN_LEV,
        lat_rows // WIN_LAT,
        WIN_LAT,
        lon_cols // WIN_LON,
        WIN_LON,
        features,
    )
    shaped = shaped.transpose(0, 2, 4, 1, 3, 5, 6)
    return shaped.reshape(-1, WIN_LEV * WIN_LAT * WIN_LON, features)


def from_windows(window_rows, level_count, lat_rows, lon_cols):
    features = window_rows.shape[-1]
    shaped = window_rows.reshape(
        level_count // WIN_LEV,
        lat_rows // WIN_LAT,
        lon_cols // WIN_LON,
        WIN_LEV,
        WIN_LAT,
        WIN_LON,
        features,
    )
    shaped = shaped.transpose(0, 3, 1, 4, 2, 5, 6)
    return shaped.reshape(level_count, lat_rows, lon_cols, features)


def merge_inputs(grid_cells):
    level_count, lat_rows, lon_cols, features = grid_cells.shape
    shaped = grid_cells.reshape(level_count, lat_rows // 2, 2, lon_cols // 2, 2, features)
    shaped = shaped.transpose(0, 1, 3, 4, 2, 5)
    shaped = shaped.reshape(level_count * (lat_rows // 2) * (lon_cols // 2), 4 * features)
    return normalize(shaped.astype(jnp.float32)).astype(jnp.bfloat16)


def roll_forward(grid_cells):
    lat_shift = WIN_LAT // 2
    lon_shift = WIN_LON // 2
    grid_cells = jnp.roll(grid_cells, -(WIN_LEV // 2), axis=0)
    incoming = from_behind(grid_cells[:, :lat_shift], "lat", -1)
    grid_cells = jnp.concatenate([grid_cells[:, lat_shift:], incoming], axis=1)
    incoming = from_behind(grid_cells[:, :, :lon_shift], "lon", -1)
    return jnp.concatenate([grid_cells[:, :, lon_shift:], incoming], axis=2)


def roll_back(grid_cells):
    lat_shift = WIN_LAT // 2
    lon_shift = WIN_LON // 2
    lat_rows = grid_cells.shape[1]
    lon_cols = grid_cells.shape[2]
    incoming = from_behind(grid_cells[:, :, lon_cols - lon_shift :], "lon", 1)
    grid_cells = jnp.concatenate([incoming, grid_cells[:, :, : lon_cols - lon_shift]], axis=2)
    incoming = from_behind(grid_cells[:, lat_rows - lat_shift :], "lat", 1)
    grid_cells = jnp.concatenate([incoming, grid_cells[:, : lat_rows - lat_shift]], axis=1)
    return jnp.roll(grid_cells, WIN_LEV // 2, axis=0)


def shards(latents, qkv_weight, proj_weight, merge_weight, bias_table, bias_index, cotangent):
    level_count, lat_rows, lon_cols, features = latents.shape
    out_width = cotangent.shape[-1]
    table = jnp.pad(bias_table, ((0, 0), (0, BUCKETS - bias_table.shape[1])))
    index = jnp.pad(bias_index, ((0, 0), (0, 2 * LANES - WINDOW)))
    tokens = to_windows(roll_forward(latents)).reshape(TOKENS, WIDTH)
    block_out, packed, probs = forward_call(tokens, table, index, qkv_weight, proj_weight)
    rolled_out = from_windows(
        block_out.reshape(WINDOWS, WINDOW, WIDTH), level_count, lat_rows, lon_cols
    )
    restored = roll_back(rolled_out)
    merge_in, norm_pull = jax.vjp(merge_inputs, restored)
    token_rows = merge_in.shape[0]
    cotangent_rows = cotangent.reshape(token_rows, out_width)
    weight = lax.all_gather(merge_weight, "lon", axis=0, tiled=True)
    merged_rows = dot(merge_in, weight).astype(BF16)
    merge_grad = dot(cotangent_rows, weight, LAST).astype(BF16)
    merged = merged_rows.reshape(level_count, lat_rows // 2, lon_cols // 2, out_width)
    restored_grad = norm_pull(merge_grad)[0]
    rolled_grad = to_windows(roll_forward(restored_grad)).reshape(TOKENS, WIDTH)
    grad_rolled, grad_table = backward_call(
        rolled_grad, tokens, packed, probs, index, qkv_weight, proj_weight
    )
    grad_latents = roll_back(
        from_windows(grad_rolled.reshape(WINDOWS, WINDOW, WIDTH), level_count, lat_rows, lon_cols)
    )
    grad_bias = lax.psum(grad_table[:, :bias_table.shape[1]], ("lon", "lat"))
    return (merged, grad_latents, grad_bias)


def solution(mesh):
    return jax.shard_map(
        shards,
        mesh=mesh,
        in_specs=(
            P(None, "lat", "lon", None),
            P(),
            P(),
            P("lon", None),
            P(),
            P(),
            P(None, "lat", "lon", None),
        ),
        out_specs=(P(None, "lat", "lon", None), P(None, "lat", "lon", None), P()),
        check_vma=False,
    )
```

time: 508 us -> 306 us (0.60)
  other arithmetic: 148 us -> 4.33 us
  local copies, waits for them, and re-layouts: 142 us -> 17.9 us
  waiting for transfers between devices: 41.9 us -> 94.3 us
  Pallas kernels: 0 us -> 48.7 us
  matrix products: 56.5 us -> 20.1 us
  starting transfers between devices: 12.1 us -> 21.9 us
    scatter-add x1 -> x0, other arithmetic: 113 us -> none  [attend(): bias_terms = jnp.take(bias_table, bias_index, axis=1)]
    gather x2 -> x0, local copies, waits for them, and re-layouts: 51.1 us -> none  [attend(): bias_terms = jnp.take(bias_table, bias_index, axis=1)]
    pallas_call x0 -> x2, Pallas kernels: none -> 48.7 us  [the longest x1 28.5 us: backward_call(): pl.pallas_call(backward_kernel, out_shape=(jax.ShapeDtypeStruct((TOKENS,...]
    dot_general x12 -> x2, matrix products: 56.5 us -> 20.1 us  [dot(): return lax.dot_general(a, b, dims, preferred_element_type=F32)]
    all_gather x1, waiting for transfers between devices: 0.02 us -> 27.4 us  [shards(): weight = lax.all_gather(merge_weight, 'lon', axis=0, tiled=True)]
    ppermute x8, waiting for transfers between devices: 41.2 us -> 66.2 us  [from_behind(): lax.ppermute(shard, axis, [(i, (i + by) % devices) for i in range(devices)])]
    reshape x7 -> x0, local copies, waits for them, and re-layouts: 20.9 us -> none  [the longest x2 11.7 us: attend(): packed = packed.reshape(num_windows, window_size, 3, head_count, head_dim)]
    unnamed x81 -> x12, local copies, waits for them, and re-layouts: 16.9 us -> 2.6 us
  transfers between devices with their start and end apart: 9 -> 9, of which waited for: 5 -> 8; matrix products, arithmetic and copies ran while one was open for 53% -> 8% of each run, Pallas kernels for 0% -> 7%
where the time goes in v1:
time: 306 us; the launch traced here: 303 us
  waiting for transfers between devices  94.3 us (31%)
  blocking collectives  81 us (26%)
  Pallas kernels  48.7 us (16%)
  starting transfers between devices  21.9 us (7%)
  matrix products  20.1 us (7%)
  local copies, waits for them, and re-layouts  17.9 us (6%)
  between operations  14.6 us (5%)
  other arithmetic  4.33 us (1%)
    psum x1, blocking collectives, shards(): grad_bias = lax.psum(grad_table[:, :bias_table.shape[1]], ('lon', 'lat'))  81 us
    ppermute x8, waiting for transfers between devices, from_behind(): lax.ppermute(shard, axis, [(i, (i + by) % devices) for i in range(devices)])  66.2 us
    pallas_call x1, Pallas kernels, backward_call(): pl.pallas_call(backward_kernel, out_shape=(jax.ShapeDtypeStruct((TOKENS,...  28.5 us
    all_gather x1, waiting for transfers between devices, shards(): weight = lax.all_gather(merge_weight, 'lon', axis=0, tiled=True)  27.4 us
    ppermute x8, starting transfers between devices, from_behind(): lax.ppermute(shard, axis, [(i, (i + by) % devices) for i in range(devices)])  21.9 us
    pallas_call x1, Pallas kernels, forward_call(): pl.pallas_call(kernel, out_shape=(jax.ShapeDtypeStruct((TOKENS, WIDTH), B...  20.2 us
    dot_general x2, matrix products, dot(): return lax.dot_general(a, b, dims, preferred_element_type=F32)  20.1 us
  transfers between devices with their start and end apart: 9, of which 8 were waited for; matrix products, arithmetic and copies ran while one was open for 8% of the time, Pallas kernels for 7%

profile of v1, /device:TPU:1, one launch (start us, length us, event | category | flops | bytes accessed | tf_op | source)
XLA Modules:
  0.0 302.8 jit_solution(15755883778799254764)
XLA Ops:
  7.2 0.7 all-gather.2.cloned.1.call-update
  7.9 1.3 slice.86
  9.2 1.4 slice.85
  10.6 0.6 fusion.10
  11.2 6.1 %collective-permute-start = (bf16[4,6,6,1024]{3,0,2,1:T(4,128)(2,1)S(1)}, bf16[4,6,6,1024]{3,0,2,1:T(4,128)(2,1)S(1)}, u32[]{:S(2)}, u32[]{:S(2)}) collective-permute-start(bf16[4,6,6,1024]{3,0,2,1:T(4,128)(2,1)S(1)} %get-tuple-element.25), channel_id=1, source_target_pairs={{0,7},{1,0},{2,1},{3,2},{4,3},{5,4},{6,5},{7,6},{8,15},{9,8},{10,9... | collective-permute-start | bytes 884744 | tf_op jit(solution)/shard_map/ppermute | solution.py:219
  17.3 5.7 %collective-permute-done = bf16[4,6,6,1024]{3,0,2,1:T(4,128)(2,1)S(1)} collective-permute-done((bf16[4,6,6,1024]{3,0,2,1:T(4,128)(2,1)S(1)}, bf16[4,6,6,1024]{3,0,2,1:T(4,128)(2,1)S(1)}, u32[]{:S(2)}, u32[]{:S(2)}) %collective-permute-start) | collective-permute-done | bytes 294944 | tf_op jit(solution)/shard_map/ppermute | solution.py:219
  23.0 0.4 fusion.9
  23.4 2.1 collective-permute-start.1
  25.6 0.6 pad.8.table_ref
  26.2 0.7 pad.9.index_ref
  26.9 9.4 %collective-permute-done.1 = bf16[4,12,3,1024]{3,0,2,1:T(4,128)(2,1)S(1)} collective-permute-done((bf16[4,12,3,1024]{3,0,2,1:T(4,128)(2,1)S(1)}, bf16[4,12,3,1024]{3,0,2,1:T(4,128)(2,1)S(1)}, u32[]{:S(2)}, u32[]{:S(2)}) %collective-permute-start.1) | collective-permute-done | bytes 294944 | tf_op jit(solution)/shard_map/ppermute | solution.py:219
  36.3 0.4 pad_maximum_fusion.9
  36.7 0.2 copy.26
  36.9 1.0 reshape_reshape_transpose_reshape.6.x_ref
  37.9 20.2 %attention_forward.1 = (bf16[288,1024]{1,0:T(8,128)(2,1)}, bf16[288,3072]{1,0:T(8,128)(2,1)}, bf16[2,16,144,144]{3,2,1,0:T(8,128)(2,1)}) custom-call(bf16[288,1024]{1,0:T(8,128)(2,1)} %reshape_reshape_transpose_reshape.6.x_ref, f32[16,768]{1,0:T(8,128)} %pad.8.table_ref, s32[144,256]{1,0:T(8,128)} %pad.9.index_ref, bf16[1024,3072]{1,0:T(8,128)(2,1)} %wqkv_ref.3, ...), custom_call_target="tpu_custom_call" | custom-call | flops 2936012800 | bytes 16777216 | tf_op jit(solution)/shard_map/attention_forward/pallas_call | solution.py:112
  58.1 1.3 reshape_transpose_reshape_reshape.6
  59.4 0.3 fusion.14
  59.7 0.1 collective-permute-start.2
  59.7 13.5 %collective-permute-done.2 = bf16[4,12,3,1024]{3,2,1,0:T(4,128)(2,1)S(1)} collective-permute-done((bf16[4,12,3,1024]{3,2,1,0:T(4,128)(2,1)S(1)}, bf16[4,12,3,1024]{3,2,1,0:T(4,128)(2,1)S(1)}, u32[]{:S(2)}, u32[]{:S(2)}) %collective-permute-start.2) | collective-permute-done | bytes 294944 | tf_op jit(solution)/shard_map/ppermute | solution.py:219
  73.3 0.2 fusion.8
  73.5 4.4 %collective-permute-start.3 = (bf16[4,6,6,1024]{3,2,1,0:T(8,128)(2,1)S(1)}, bf16[4,6,6,1024]{3,2,1,0:T(8,128)(2,1)S(1)}, u32[]{:S(2)}, u32[]{:S(2)}) collective-permute-start(bf16[4,6,6,1024]{3,2,1,0:T(8,128)(2,1)S(1)} %fusion.8), channel_id=1, source_target_pairs={{0,1},{1,2},{2,3},{3,4},{4,5},{5,6},{6,7},{7,0},{8,9},{9,10},{10,1... | collective-permute-start | bytes 884744 | tf_op jit(solution)/shard_map/ppermute | solution.py:219
  77.9 0.3 copy.31
  78.1 1.0 reshape.70
  79.1 18.5 %collective-permute-done.3 = bf16[4,6,6,1024]{3,2,1,0:T(8,128)(2,1)S(1)} collective-permute-done((bf16[4,6,6,1024]{3,2,1,0:T(8,128)(2,1)S(1)}, bf16[4,6,6,1024]{3,2,1,0:T(8,128)(2,1)S(1)}, u32[]{:S(2)}, u32[]{:S(2)}) %collective-permute-start.3) | collective-permute-done | bytes 294944 | tf_op jit(solution)/shard_map/ppermute | solution.py:219
  97.6 0.3 fusion.3
  97.9 0.8 copy.27
  98.7 0.3 reduce_sum.35
  98.9 0.9 copy.28
  99.8 1.0 reshape.72
  100.9 0.1 copy.29
  101.0 0.5 multiply_reduce_fusion.1
  101.5 0.1 copy.30
  101.6 0.1 add.24
  101.7 0.1 div.21
  101.8 27.4 %all-gather.2.cloned.1.call-done = bf16[4096,2048]{1,0:T(8,128)(2,1)} async-done(((bf16[128,2048]{1,0:T(8,128)(2,1)}), bf16[4096,2048]{1,0:T(8,128)(2,1)}) %all-gather.2.cloned.1.call-update) | async-done | bytes 16777232 | tf_op jit(solution)/shard_map/all_gather | solution.py:303
  129.2 11.2 %multiply_reduce_fusion = (f32[72]{0:T(128)S(1)}, f32[72,4096]{1,0:T(8,128)S(1)}) fusion(f32[72,4096]{1,0:T(8,128)S(1)} %reshape.72, f32[72]{0:T(128)S(1)} %div.21, bf16[72,2048]{1,0:T(8,128)(2,1)} %reshape.70, bf16[4096,2048]{1,0:T(8,128)(2,1)} %all-gather.2.cloned.1.call-done), kind=kOutput, calls=%fused_computation.5 | convolution fusion | flops 1209433984 | bytes 19432000 | tf_op jit(solution)/shard_map/dot_general | solution.py:30
  140.4 0.4 fusion.11
  140.8 0.1 add_convert_fusion
  141.0 0.4 reshape.71
  141.4 0.1 slice.121
  141.5 0.3 slice.120
  141.9 0.3 copy.32
  142.2 0.1 copy.33
  142.4 0.2 slice.98
  142.7 5.0 %collective-permute-start.4 = (bf16[4,6,6,1024]{3,2,1,0:T(8,128)(2,1)S(1)}, bf16[4,6,6,1024]{3,2,1,0:T(8,128)(2,1)S(1)}, u32[]{:S(2)}, u32[]{:S(2)}) collective-permute-start(bf16[4,6,6,1024]{3,2,1,0:T(8,128)(2,1)S(1)} %get-tuple-element.31), channel_id=1, source_target_pairs={{0,7},{1,0},{2,1},{3,2},{4,3},{5,4},{6,5},{7,6},{8,15},{9,8},{10,9... | collective-permute-start | bytes 884744 | tf_op jit(solution)/shard_map/ppermute | solution.py:219
  147.7 8.2 %collective-permute-done.4 = bf16[4,6,6,1024]{3,2,1,0:T(8,128)(2,1)S(1)} collective-permute-done((bf16[4,6,6,1024]{3,2,1,0:T(8,128)(2,1)S(1)}, bf16[4,6,6,1024]{3,2,1,0:T(8,128)(2,1)S(1)}, u32[]{:S(2)}, u32[]{:S(2)}) %collective-permute-start.4) | collective-permute-done | bytes 294944 | tf_op jit(solution)/shard_map/ppermute | solution.py:219
  155.9 0.3 fusion.7
  156.2 1.4 collective-permute-start.5
  157.6 6.1 %collective-permute-done.5 = bf16[4,12,3,1024]{3,2,1,0:T(4,128)(2,1)S(1)} collective-permute-done((bf16[4,12,3,1024]{3,2,1,0:T(4,128)(2,1)S(1)}, bf16[4,12,3,1024]{3,2,1,0:T(4,128)(2,1)S(1)}, u32[]{:S(2)}, u32[]{:S(2)}) %collective-permute-start.5) | collective-permute-done | bytes 294944 | tf_op jit(solution)/shard_map/ppermute | solution.py:219
  163.7 0.4 pad_maximum_fusion.8
  164.1 1.0 reshape_reshape_transpose_reshape.7.grad_ref
  165.1 28.5 %attention_backward.1 = (bf16[288,1024]{1,0:T(8,128)(2,1)}, f32[16,768]{1,0:T(8,128)}) custom-call(bf16[288,1024]{1,0:T(8,128)(2,1)} %reshape_reshape_transpose_reshape.7.grad_ref, bf16[288,1024]{1,0:T(8,128)(2,1)} %reshape_reshape_transpose_reshape.6.x_ref, bf16[288,3072]{1,0:T(8,128)(2,1)} %get-tuple-element.9.packed_ref, ...), custom_call_target="tpu_custom_call" | custom-call | flops 3565158400 | bytes 16777216 | tf_op jit(solution)/shard_map/attention_backward/pallas_call | solution.py:197
  193.6 1.3 reshape_transpose_reshape_reshape.7
  194.9 0.3 fusion.12
  195.2 0.1 collective-permute-start.6
  195.3 4.7 %collective-permute-done.6 = bf16[4,12,3,1024]{3,2,1,0:T(4,128)(2,1)S(1)} collective-permute-done((bf16[4,12,3,1024]{3,2,1,0:T(4,128)(2,1)S(1)}, bf16[4,12,3,1024]{3,2,1,0:T(4,128)(2,1)S(1)}, u32[]{:S(2)}, u32[]{:S(2)}) %collective-permute-start.6) | collective-permute-done | bytes 294944 | tf_op jit(solution)/shard_map/ppermute | solution.py:219
  200.0 0.2 fusion.6
  200.2 2.8 collective-permute-start.7
  203.0 8.9 %convolution_convert_fusion.1 = bf16[72,2048]{1,0:T(8,128)(2,1)S(1)} fusion(bf16[4096,2048]{1,0:T(8,128)(2,1)} %all-gather.2.cloned.1.call-done, f32[72,4096]{1,0:T(8,128)S(1)} %reshape.72, f32[72]{0:T(128)S(1)} %get-tuple-element.37, f32[72]{0:T(128)S(1)} %div.21), kind=kOutput, calls=%fused_computation.2 | convolution fusion | flops 1208991744 | bytes 18252352 | tf_op jit(solution)/shard_map/dot_general | solution.py:30
  211.9 0.2 reshape.69
  212.1 1.0 copy.34
  213.1 81.0 %psum.7 = f32[16,759]{1,0:T(8,128)} all-reduce(f32[16,759]{1,0:T(8,128)S(1)} %bitcast.13), channel_id=1, replica_groups=mesh['lon'=32,'lat'=8] {'lon','lat'}, use_global_device_ids=true, to_apply=%region_4.5 | all-reduce | flops 12144 | bytes 97152 | tf_op jit(solution)/shard_map/psum | solution.py:315
  294.1 0.3 fusion.1
  294.4 1.3 copy.35
  (18 shorter events, 0.3 us)
Async XLA Ops:
  7.2 122.0 %all-gather.2.cloned.1.call-start = ((), (), s32[]{:S(2)}) async-start(), calls=%async_computation | async-start | bytes 17301504 | tf_op jit(solution)/shard_map/all_gather | solution.py:303
  10.6 15.0 %copy-start.2 = (f32[16,759]{1,0:T(8,128)S(1)}, f32[16,759]{1,0:T(8,128)}, u32[]{:S(2)}) copy-start(f32[16,759]{1,0:T(8,128)} %param.11) | copy-start | bytes 145732
  10.6 15.6 %copy-start.1 = (s32[144,144]{1,0:T(8,128)S(1)}, s32[144,144]{1,0:T(8,128)}, u32[]{:S(2)}) copy-start(s32[144,144]{1,0:T(8,128)} %param.12) | copy-start | bytes 248836
  11.2 11.8 %collective-permute-start = (bf16[4,6,6,1024]{3,0,2,1:T(4,128)(2,1)S(1)}, bf16[4,6,6,1024]{3,0,2,1:T(4,128)(2,1)S(1)}, u32[]{:S(2)}, u32[]{:S(2)}) collective-permute-start(bf16[4,6,6,1024]{3,0,2,1:T(4,128)(2,1)S(1)} %get-tuple-element.25), channel_id=1, source_target_pairs={{0,7},{1,0},{2,1},{3,2},{4,3},{5,4},{6,5},{7,6},{8,15},{9,8},{10,9... | collective-permute-start | bytes 884744 | tf_op jit(solution)/shard_map/ppermute | solution.py:219
  23.4 12.9 %collective-permute-start.1 = (bf16[4,12,3,1024]{3,0,2,1:T(4,128)(2,1)S(1)}, bf16[4,12,3,1024]{3,0,2,1:T(4,128)(2,1)S(1)}, u32[]{:S(2)}, u32[]{:S(2)}) collective-permute-start(bf16[4,12,3,1024]{3,0,2,1:T(4,128)(2,1)S(1)} %get-tuple-element.35), channel_id=1, source_target_pairs={{0,248},{8,0},{16,8},{24,16},{32,24},{40,32},{48,40},{56,48},{64,5... | collective-permute-start | bytes 884744 | tf_op jit(solution)/shard_map/ppermute | solution.py:219
  59.4 18.5 %copy-start = (bf16[4,6,3,2048]{3,0,2,1:T(4,128)(2,1)S(1)}, bf16[4,6,3,2048]{3,0,2,1:T(4,128)(2,1)}, u32[]{:S(2)}) copy-start(bf16[4,6,3,2048]{3,0,2,1:T(4,128)(2,1)} %param.13) | copy-start | bytes 884740
  59.7 13.6 %collective-permute-start.2 = (bf16[4,12,3,1024]{3,2,1,0:T(4,128)(2,1)S(1)}, bf16[4,12,3,1024]{3,2,1,0:T(4,128)(2,1)S(1)}, u32[]{:S(2)}, u32[]{:S(2)}) collective-permute-start(bf16[4,12,3,1024]{3,2,1,0:T(4,128)(2,1)S(1)} %get-tuple-element.33), channel_id=1, source_target_pairs={{0,8},{8,16},{16,24},{24,32},{32,40},{40,48},{48,56},{56,64},{64,7... | collective-permute-start | bytes 884744 | tf_op jit(solution)/shard_map/ppermute | solution.py:219
  73.5 24.1 %collective-permute-start.3 = (bf16[4,6,6,1024]{3,2,1,0:T(8,128)(2,1)S(1)}, bf16[4,6,6,1024]{3,2,1,0:T(8,128)(2,1)S(1)}, u32[]{:S(2)}, u32[]{:S(2)}) collective-permute-start(bf16[4,6,6,1024]{3,2,1,0:T(8,128)(2,1)S(1)} %fusion.8), channel_id=1, source_target_pairs={{0,1},{1,2},{2,3},{3,4},{4,5},{5,6},{6,7},{7,0},{8,9},{9,10},{10,1... | collective-permute-start | bytes 884744 | tf_op jit(solution)/shard_map/ppermute | solution.py:219
  142.7 13.2 %collective-permute-start.4 = (bf16[4,6,6,1024]{3,2,1,0:T(8,128)(2,1)S(1)}, bf16[4,6,6,1024]{3,2,1,0:T(8,128)(2,1)S(1)}, u32[]{:S(2)}, u32[]{:S(2)}) collective-permute-start(bf16[4,6,6,1024]{3,2,1,0:T(8,128)(2,1)S(1)} %get-tuple-element.31), channel_id=1, source_target_pairs={{0,7},{1,0},{2,1},{3,2},{4,3},{5,4},{6,5},{7,6},{8,15},{9,8},{10,9... | collective-permute-start | bytes 884744 | tf_op jit(solution)/shard_map/ppermute | solution.py:219
  156.2 7.5 %collective-permute-start.5 = (bf16[4,12,3,1024]{3,2,1,0:T(4,128)(2,1)S(1)}, bf16[4,12,3,1024]{3,2,1,0:T(4,128)(2,1)S(1)}, u32[]{:S(2)}, u32[]{:S(2)}) collective-permute-start(bf16[4,12,3,1024]{3,2,1,0:T(4,128)(2,1)S(1)} %get-tuple-element.29), channel_id=1, source_target_pairs={{0,248},{8,0},{16,8},{24,16},{32,24},{40,32},{48,40},{56,48},{64,5... | collective-permute-start | bytes 884744 | tf_op jit(solution)/shard_map/ppermute | solution.py:219
  195.2 4.8 %collective-permute-start.6 = (bf16[4,12,3,1024]{3,2,1,0:T(4,128)(2,1)S(1)}, bf16[4,12,3,1024]{3,2,1,0:T(4,128)(2,1)S(1)}, u32[]{:S(2)}, u32[]{:S(2)}) collective-permute-start(bf16[4,12,3,1024]{3,2,1,0:T(4,128)(2,1)S(1)} %get-tuple-element.27), channel_id=1, source_target_pairs={{0,8},{8,16},{16,24},{24,32},{32,40},{40,48},{48,56},{56,64},{64,7... | collective-permute-start | bytes 884744 | tf_op jit(solution)/shard_map/ppermute | solution.py:219
  200.2 12.8 %copy-start.3 = (f32[16,768]{1,0:T(8,128)S(1)}, f32[16,768]{1,0:T(8,128)}, u32[]{:S(2)}) copy-start(f32[16,768]{1,0:T(8,128)} %get-tuple-element.12) | copy-start | bytes 147460
  200.2 93.9 %collective-permute-start.7 = (bf16[4,6,6,1024]{3,2,1,0:T(8,128)(2,1)S(1)}, bf16[4,6,6,1024]{3,2,1,0:T(8,128)(2,1)S(1)}, u32[]{:S(2)}, u32[]{:S(2)}) collective-permute-start(bf16[4,6,6,1024]{3,2,1,0:T(8,128)(2,1)S(1)} %fusion.6), channel_id=1, source_target_pairs={{0,1},{1,2},{2,3},{3,4},{4,5},{5,6},{6,7},{7,0},{8,9},{9,10},{10,1... | collective-permute-start | bytes 884744 | tf_op jit(solution)/shard_map/ppermute | solution.py:219
Sparse Core Ops, SparseCore 0:
  9.9 119.2 all-gather.1

commit v2 on v1

v2 whole, which is shorter than its diff:
```python
import jax
import jax.numpy as jnp
import numpy as np
from jax import lax
from jax.experimental import pallas as pl
from jax.experimental.pallas import tpu as pltpu
from jax.sharding import PartitionSpec as P

EPS = 1e-05
MASKED = -1e30
HEADS = 16
PAIRS = 8
HEAD_DIM = 64
WINDOW = 144
WINDOWS = 2
TOKENS = WINDOW * WINDOWS
WIDTH = 1024
OUT = 2048
BUCKETS = 768
LANES = 128
SPLIT = 256
TEAM = 4
RING = 8
BANDS = 8
PIECE = 128
CELLS = 72
SLAB = 80
F32 = jnp.float32
BF16 = jnp.bfloat16
LAST = (((1,), (1,)), ((), ()))
FIRST = (((0,), (0,)), ((), ()))
MESH = pl.DeviceIdType.MESH


def dot(a, b, dims=(((1,), (0,)), ((), ()))):
    return lax.dot_general(a, b, dims, preferred_element_type=F32)


def quad_row(level, row, col):
    quad = 2 * (row // 6) + col // 3
    return quad * SLAB + level * 18 + (row % 6) * 3 + col % 3


def orders():
    natural = np.zeros((4 * SLAB, TOKENS), np.float32)
    window = np.zeros((TOKENS, 4 * SLAB), np.float32)
    merge = np.zeros((TOKENS, 4 * SLAB), np.float32)
    for level in range(4):
        for row in range(12):
            for col in range(6):
                cell = (level * 12 + row) * 6 + col
                place = quad_row(level, row, col)
                natural[place, cell] = 1
                source = quad_row((level + 1) % 4, (row + 6) % 12, (col + 3) % 6)
                window[cell, source] = 1
                spot = 2 * (col % 2) + row % 2
                merge[spot * CELLS + (level * 6 + row // 2) * 3 + col // 2, place] = 1
    return [jnp.asarray(m, BF16) for m in (natural, window, window.T, merge, merge.T, natural.T)]


def stats(values):
    average = jnp.mean(values, axis=-1, keepdims=True)
    centered = values - average
    variance = jnp.mean(centered * centered, axis=-1, keepdims=True)
    return centered, lax.rsqrt(variance + EPS)


def half_mask(shape, half):
    lane = lax.broadcasted_iota(jnp.int32, shape, 1)
    return (lane >= HEAD_DIM) if half else (lane < HEAD_DIM)


def region_code(shape, axis, window, is_last):
    token = lax.broadcasted_iota(jnp.int32, shape, axis)
    level = (token >= 72).astype(jnp.int32)
    row = token - 72 * level
    late = (row >= 36).astype(jnp.int32)
    return late * is_last + (2 * level if window == 1 else 0)


def allowed_pairs(window, is_last):
    shape = (WINDOW, WINDOW)
    return region_code(shape, 0, window, is_last) == region_code(shape, 1, window, is_last)


def gather_bias(table_ref, index_ref, head):
    tiles = []
    for tile in range(2):
        index = index_ref[:, tile * LANES:(tile + 1) * LANES]
        low = index & (LANES - 1)
        high = index >> 7
        found = None
        for chunk in range(BUCKETS // LANES):
            row = table_ref[pl.ds(head, 1), chunk * LANES:(chunk + 1) * LANES]
            spread = jnp.broadcast_to(row, (WINDOW, LANES))
            part = jnp.take_along_axis(spread, low, axis=1, mode="promise_in_bounds")
            found = part if found is None else jnp.where(high == chunk, part, found)
        tiles.append(found)
    return jnp.concatenate(tiles, axis=1)[:, :WINDOW]


def attend_pair(pair, is_last, table_ref, index_ref, packed, probs_ref, attended):
    base = pl.multiple_of(pair * LANES, LANES)
    bias = [gather_bias(table_ref, index_ref, 2 * pair + half) for half in range(2)]
    masks = [half_mask((WINDOW, LANES), half) for half in range(2)]
    zero = jnp.zeros((WINDOW, LANES), BF16)
    for window in range(WINDOWS):
        rows = slice(window * WINDOW, (window + 1) * WINDOW)
        allowed = allowed_pairs(window, is_last)
        query = packed[rows, pl.ds(base, LANES)] * jnp.array(HEAD_DIM ** -0.5, BF16)
        key = packed[rows, pl.ds(WIDTH + base, LANES)]
        value = packed[rows, pl.ds(2 * WIDTH + base, LANES)]
        mixed = None
        for half in range(2):
            scores = dot(jnp.where(masks[half], query, zero), key, LAST)
            scores = jnp.where(allowed, scores + bias[half], MASKED)
            weights = jnp.exp(scores - jnp.max(scores, axis=-1, keepdims=True))
            probs = (weights * (1.0 / jnp.sum(weights, axis=-1, keepdims=True))).astype(BF16)
            probs_ref[window, 2 * pair + half] = probs
            term = dot(probs, jnp.where(masks[half], value, zero))
            mixed = term if mixed is None else mixed + term
        attended[rows, pl.ds(base, LANES)] = mixed.astype(BF16)


def unattend_pair(pair, packed, probs_ref, datt, dpacked, dmain, dtail):
    base = pl.multiple_of(pair * LANES, LANES)
    scale = jnp.array(HEAD_DIM ** -0.5, BF16)
    masks = [half_mask((WINDOW, LANES), half) for half in range(2)]
    zero = jnp.zeros((WINDOW, LANES), BF16)
    sums = [None, None]
    for window in range(WINDOWS):
        rows = slice(window * WINDOW, (window + 1) * WINDOW)
        query = packed[rows, pl.ds(base, LANES)] * scale
        key = packed[rows, pl.ds(WIDTH + base, LANES)] * scale
        value = packed[rows, pl.ds(2 * WIDTH + base, LANES)]
        out_grad = datt[rows, pl.ds(base, LANES)]
        dquery, dkey, dvalue = None, None, None
        for half in range(2):
            grad = jnp.where(masks[half], out_grad, zero)
            probs = probs_ref[window, 2 * pair + half]
            wide = probs.astype(F32)
            product = wide * dot(grad, value, LAST)
            ds = product - wide * jnp.sum(product, axis=-1, keepdims=True)
            sums[half] = ds if sums[half] is None else sums[half] + ds
            narrow = ds.astype(BF16)
            one = dot(narrow, jnp.where(masks[half], key, zero))
            two = dot(narrow, jnp.where(masks[half], query, zero), FIRST)
            three = dot(probs, grad, FIRST)
            dquery = one if dquery is None else dquery + one
            dkey = two if dkey is None else dkey + two
            dvalue = three if dvalue is None else dvalue + three
        dpacked[rows, pl.ds(base, LANES)] = dquery.astype(BF16)
        dpacked[rows, pl.ds(WIDTH + base, LANES)] = dkey.astype(BF16)
        dpacked[rows, pl.ds(2 * WIDTH + base, LANES)] = dvalue.astype(BF16)
    for half in range(2):
        total = jnp.concatenate([sums[half], jnp.zeros((WINDOW, 2 * LANES - WINDOW), F32)], axis=1)
        for tile, store in enumerate((dmain, dtail)):
            cols = slice(tile * LANES, (tile + 1) * LANES)
            store[pl.ds(2 * pair + half, WINDOW, stride=HEADS), :] = total[:, cols]


def scatter_table(index_ref, dmain, dtail):
    def scatter_row(row, total):
        here = pl.ds(pl.multiple_of(row * HEADS, HEADS), HEADS)
        block = jnp.concatenate([dmain[here, :], dtail[here, :]], axis=1)
        index = index_ref[pl.ds(row, 1), :]
        low = index & (SPLIT - 1)
        high = index >> 8
        parts = jnp.concatenate(
            [jnp.where(high == part, block, 0.0) for part in range(BUCKETS // SPLIT)], axis=0
        )
        coarse = parts.astype(BF16)
        fine = (parts - coarse.astype(F32)).astype(BF16)
        bucket = lax.broadcasted_iota(jnp.int32, (SPLIT, 2 * LANES), 0)
        hot = jnp.where(bucket == low, 1.0, 0.0).astype(BF16)
        return total + dot(jnp.concatenate([coarse, fine], axis=0), hot, LAST)

    rows = HEADS * (BUCKETS // SPLIT)
    total = lax.fori_loop(0, WINDOW, scatter_row, jnp.zeros((2 * rows, SPLIT), F32), unroll=4)
    total = total[:rows] + total[rows:]
    return jnp.concatenate([total[part * HEADS:(part + 1) * HEADS] for part in range(BUCKETS // SPLIT)], axis=1)


def pad_rows(values):
    return jnp.concatenate([values, jnp.zeros((SLAB - CELLS, values.shape[1]), F32)], axis=0).astype(BF16)


def kernel(
    nat2quad, quad2win, win2quad, quad2merge, merge2quad, quad2nat,
    x_ref, table_ref, index_ref, cot_hbm, piece_hbm, wqkv_hbm, wproj_hbm,
    merged_ref, grad_ref, bias_ref,
    wqkv, wproj, wbuf, cots, sent, landed, tokens, normed, packed, probs, attended,
    hats, gsend, grecv, msend, mrecv, psend, precv, datt, dpacked, dmain, dtail,
    sum_team, sum_ring, sum_bands, local_sems, send_sems, recv_sems,
):
    lon = lax.axis_index("lon")
    lat = lax.axis_index("lat")
    ring = lon // TEAM
    member = lax.rem(lon, TEAM)
    lons = RING * TEAM
    is_last = (lat == BANDS - 1).astype(jnp.int32)

    def team_peer(step):
        return {"lon": ring * TEAM + lax.rem(member + step, TEAM), "lat": lat}

    def ring_peer(step):
        return {"lon": lax.rem(ring + step, RING) * TEAM + member, "lat": lat}

    def band_peer(step):
        return {"lon": lon, "lat": lax.rem(lat + step, BANDS)}

    def near(rows, cols):
        return {"lon": lax.rem(lon + cols + lons, lons), "lat": lax.rem(lat + rows + BANDS, BANDS)}

    peers = [team_peer(step) for step in range(1, TEAM)]
    peers += [ring_peer(step) for step in range(1, RING)]
    peers += [band_peer(step) for step in range(1, BANDS)]
    peers += [near(0, 1), near(0, -1), near(1, 1), near(-1, -1)]

    loads = [
        pltpu.make_async_copy(wqkv_hbm, wqkv, local_sems.at[0]),
        pltpu.make_async_copy(wproj_hbm, wproj, local_sems.at[1]),
        pltpu.make_async_copy(cot_hbm, cots.at[member], local_sems.at[2]),
        pltpu.make_async_copy(piece_hbm, wbuf.at[ring], local_sems.at[3]),
    ]
    for load in loads:
        load.start()

    barrier = pltpu.get_barrier_semaphore()
    for peer in peers:
        pl.semaphore_signal(barrier, inc=1, device_id=peer, device_id_type=MESH)

    copies = []

    def remote(source, target, peer):
        slot = len(copies)
        copy = pltpu.make_async_remote_copy(
            src_ref=source, dst_ref=target, send_sem=send_sems.at[slot], recv_sem=recv_sems.at[slot],
            device_id=peer, device_id_type=MESH,
        )
        copies.append(copy)
        return copy

    def exchange(stage, side):
        moves = []
        for quad, (rows, cols) in enumerate(((1, 1), (1, 0), (0, 1))):
            moves.append(remote(sent.at[stage, quad], landed.at[stage, quad], near(side * rows, side * cols)))
        return moves

    def fill(stage, order, values):
        for quad in range(4):
            rows = dot(order[quad * SLAB:(quad + 1) * SLAB, :], values).astype(BF16)
            if quad == 3:
                landed[stage, quad] = rows
            else:
                sent[stage, quad] = rows

    def arrived(stage, order):
        return dot(order[...], landed[stage].reshape(4 * SLAB, WIDTH))

    fill(0, nat2quad, x_ref[...])
    pl.semaphore_wait(barrier, len(peers))

    first = exchange(0, -1)
    for copy in first:
        copy.start()

    half = PIECE // 2
    ahead, behind = [], []
    for step in range(4):
        up = lax.rem(ring - step + RING, RING)
        down = lax.rem(ring + step, RING)
        if step == 0:
            ahead.append(remote(piece_hbm, wbuf.at[ring], ring_peer(1)))
            behind.append(remote(piece_hbm, wbuf.at[ring], ring_peer(RING - 1)))
        elif step < 3:
            ahead.append(remote(wbuf.at[up], wbuf.at[up], ring_peer(1)))
            behind.append(remote(wbuf.at[down], wbuf.at[down], ring_peer(RING - 1)))
        else:
            top, bottom = pl.ds(0, half), pl.ds(half, half)
            ahead.append(remote(wbuf.at[up, top], wbuf.at[up, top], ring_peer(1)))
            behind.append(remote(wbuf.at[down, bottom], wbuf.at[down, bottom], ring_peer(RING - 1)))

    def ring_step(step):
        if step > 0:
            ahead[step - 1].wait_recv()
            behind[step - 1].wait_recv()
        if step < 4:
            ahead[step].start()
            behind[step].start()

    spread = [remote(cot_hbm, cots.at[member], team_peer(step)) for step in range(1, TEAM)]
    for copy in spread:
        copy.start()
    ring_step(0)

    for copy in first:
        copy.wait_recv()
    values = arrived(0, quad2win)
    tokens[...] = values.astype(BF16)
    centered, inverse = stats(values)
    normed[...] = (centered * inverse).astype(BF16)
    loads[0].wait()
    for part in range(12):
        cols = slice(part * 256, (part + 1) * 256)
        packed[:, cols] = dot(normed[...], wqkv[:, cols]).astype(BF16)

    def attend_step(pair, carry):
        attend_pair(pair, is_last, table_ref, index_ref, packed, probs, attended)
        return carry

    ring_step(1)
    lax.fori_loop(0, PAIRS, attend_step, 0, unroll=PAIRS)
    ring_step(2)
    loads[1].wait()
    block = tokens[...].astype(F32) + dot(attended[...], wproj[...])
    fill(1, win2quad, block.astype(BF16))
    second = exchange(1, 1)
    for copy in second:
        copy.start()

    for copy in spread:
        copy.wait_recv()
    loads[2].wait()
    loads[3].wait()

    def merge_grad(spot):
        rows = dot(cots[...].reshape(TEAM * SLAB, OUT), wbuf[spot], LAST).astype(BF16)
        here = pl.ds(pl.multiple_of(spot * PIECE, PIECE), PIECE)
        gsend[:, :, here] = rows.reshape(TEAM, SLAB, PIECE)

    def merge_both(step):
        merge_grad(lax.rem(ring - step + RING, RING))
        merge_grad(lax.rem(ring + step, RING))

    merge_grad(ring)
    merge_both(1)
    merge_both(2)

    for copy in second:
        copy.wait_recv()
    slabs = arrived(1, quad2merge)
    parts = [slabs[spot * CELLS:(spot + 1) * CELLS] for spot in range(4)]
    total = sum(jnp.sum(part, axis=-1, keepdims=True) for part in parts)
    average = total * (1.0 / (4 * WIDTH))
    parts = [part - average for part in parts]
    total = sum(jnp.sum(part * part, axis=-1, keepdims=True) for part in parts)
    merge_inverse = lax.rsqrt(total * (1.0 / (4 * WIDTH)) + EPS)
    for spot in range(4):
        hat = parts[spot] * merge_inverse
        hats[spot] = hat
        rows = pad_rows(hat)
        for block_id in range(8):
            target = (2 * spot + block_id // 4) * PIECE
            msend[block_id % 4, :, target:target + PIECE] = rows[:, block_id * PIECE:(block_id + 1) * PIECE]
    mrecv[member] = msend[member]
    inputs = [
        remote(msend.at[lax.rem(member + step, TEAM)], mrecv.at[member], team_peer(step))
        for step in range(1, TEAM)
    ]
    for copy in inputs:
        copy.start()

    ring_step(3)
    merge_both(3)
    ring_step(4)
    merge_grad(lax.rem(ring + 4, RING))
    grecv[member] = gsend[member]
    grads = [
        remote(gsend.at[lax.rem(member + step, TEAM)], grecv.at[member], team_peer(step))
        for step in range(1, TEAM)
    ]
    for copy in grads:
        copy.start()

    for copy in inputs:
        copy.wait_recv()
    for part in range(8):
        cols = slice(part * 256, (part + 1) * 256)
        rows = dot(mrecv[...].reshape(TEAM * SLAB, WIDTH), wbuf[:, :, cols].reshape(RING * PIECE, 256))
        psend[:, :, cols] = rows.astype(BF16).reshape(TEAM, SLAB, 256)
    precv[member] = psend[member]

    for copy in grads:
        copy.wait_recv()
    slopes = []
    for spot in range(4):
        blocks = [
            grecv[block_id % 4, :, (2 * spot + block_id // 4) * PIECE:(2 * spot + block_id // 4 + 1) * PIECE]
            for block_id in range(8)
        ]
        slopes.append(jnp.concatenate(blocks, axis=1).astype(F32)[:CELLS])
    mean_slope = sum(jnp.sum(s, axis=-1, keepdims=True) for s in slopes) * (1.0 / (4 * WIDTH))
    mean_tilt = sum(
        jnp.sum(s * hats[spot], axis=-1, keepdims=True) for spot, s in enumerate(slopes)
    ) * (1.0 / (4 * WIDTH))
    slopes = [merge_inverse * (s - mean_slope - hats[spot] * mean_tilt) for spot, s in enumerate(slopes)]
    fill(2, merge2quad, jnp.concatenate(slopes, axis=0).astype(BF16))
    third = exchange(2, -1)
    for copy in third:
        copy.start()
    partials = [
        remote(psend.at[lax.rem(member + step, TEAM)], precv.at[member], team_peer(step))
        for step in range(1, TEAM)
    ]
    for copy in partials:
        copy.start()

    for copy in third:
        copy.wait_recv()
    attended[...] = arrived(2, quad2win).astype(BF16)
    datt[...] = dot(attended[...], wproj[...], LAST).astype(BF16)

    def unattend_step(pair, carry):
        unattend_pair(pair, packed, probs, datt, dpacked, dmain, dtail)
        return carry

    lax.fori_loop(0, PAIRS, unattend_step, 0, unroll=PAIRS)
    sum_team[member] = scatter_table(index_ref, dmain, dtail)
    team_sums = [remote(sum_team.at[member], sum_team.at[member], team_peer(step)) for step in range(1, TEAM)]
    for copy in team_sums:
        copy.start()

    dnormed = dot(dpacked[...], wqkv[...], LAST).astype(BF16).astype(F32)
    centered, inverse = stats(tokens[...].astype(F32))
    hat = centered * inverse
    slope = jnp.mean(dnormed * hat, axis=-1, keepdims=True)
    inner = inverse * (dnormed - jnp.mean(dnormed, axis=-1, keepdims=True) - hat * slope)
    fill(3, win2quad, (attended[...].astype(F32) + inner).astype(BF16))
    fourth = exchange(3, 1)
    for copy in fourth:
        copy.start()

    for copy in team_sums:
        copy.wait_recv()
    sum_ring[ring] = sum_team[0] + sum_team[1] + sum_team[2] + sum_team[3]
    ring_sums = [remote(sum_ring.at[ring], sum_ring.at[ring], ring_peer(step)) for step in range(1, RING)]
    for copy in ring_sums:
        copy.start()

    for copy in partials:
        copy.wait_recv()
    for part in range(8):
        cols = slice(part * 256, (part + 1) * 256)
        total = precv[0, :, cols].astype(F32)
        for peer in range(1, TEAM):
            total = total + precv[peer, :, cols].astype(F32)
        merged_ref[:, cols] = total.astype(BF16)

    for copy in ring_sums:
        copy.wait_recv()
    total = sum_ring[0]
    for peer in range(1, RING):
        total = total + sum_ring[peer]
    sum_bands[lat] = total
    band_sums = [remote(sum_bands.at[lat], sum_bands.at[lat], band_peer(step)) for step in range(1, BANDS)]
    for copy in band_sums:
        copy.start()

    for copy in fourth:
        copy.wait_recv()
    grad_ref[...] = arrived(3, quad2nat).astype(BF16)

    for copy in band_sums:
        copy.wait_recv()
    total = sum_bands[0]
    for peer in range(1, BANDS):
        total = total + sum_bands[peer]
    bias_ref[...] = total
    for copy in copies:
        copy.wait_send()


COPIES = 12 + 8 + 4 * 3 + 3 + 7 + 7


def fused(x, table, index, cot, piece, wqkv, wproj):
    consts = orders()
    vmem = pl.BlockSpec(memory_space=pltpu.VMEM)
    anywhere = pl.BlockSpec(memory_space=pl.ANY)
    return pl.pallas_call(
        kernel,
        out_shape=(
            jax.ShapeDtypeStruct((SLAB, OUT), BF16),
            jax.ShapeDtypeStruct((TOKENS, WIDTH), BF16),
            jax.ShapeDtypeStruct((HEADS, BUCKETS), F32),
        ),
        in_specs=[vmem] * 9 + [anywhere] * 4,
        out_specs=[vmem] * 3,
        scratch_shapes=[
            pltpu.VMEM((WIDTH, 3 * WIDTH), BF16),
            pltpu.VMEM((WIDTH, WIDTH), BF16),
            pltpu.VMEM((RING, PIECE, OUT), BF16),
            pltpu.VMEM((TEAM, SLAB, OUT), BF16),
            pltpu.VMEM((4, 3, SLAB, WIDTH), BF16),
            pltpu.VMEM((4, 4, SLAB, WIDTH), BF16),
            pltpu.VMEM((TOKENS, WIDTH), BF16),
            pltpu.VMEM((TOKENS, WIDTH), BF16),
            pltpu.VMEM((TOKENS, 3 * WIDTH), BF16),
            pltpu.VMEM((WINDOWS, HEADS, WINDOW, WINDOW), BF16),
            pltpu.VMEM((TOKENS, WIDTH), BF16),
            pltpu.VMEM((4, CELLS, WIDTH), F32),
            pltpu.VMEM((TEAM, SLAB, WIDTH), BF16),
            pltpu.VMEM((TEAM, SLAB, WIDTH), BF16),
            pltpu.VMEM((TEAM, SLAB, WIDTH), BF16),
            pltpu.VMEM((TEAM, SLAB, WIDTH), BF16),
            pltpu.VMEM((TEAM, SLAB, OUT), BF16),
            pltpu.VMEM((TEAM, SLAB, OUT), BF16),
            pltpu.VMEM((TOKENS, WIDTH), BF16),
            pltpu.VMEM((TOKENS, 3 * WIDTH), BF16),
            pltpu.VMEM((WINDOW * HEADS, LANES), F32),
            pltpu.VMEM((WINDOW * HEADS, LANES), F32),
            pltpu.VMEM((TEAM, HEADS, BUCKETS), F32),
            pltpu.VMEM((RING, HEADS, BUCKETS), F32),
            pltpu.VMEM((BANDS, HEADS, BUCKETS), F32),
            pltpu.SemaphoreType.DMA((4,)),
            pltpu.SemaphoreType.DMA((COPIES,)),
            pltpu.SemaphoreType.DMA((COPIES,)),
        ],
        compiler_params=pltpu.CompilerParams(
            collective_id=0, has_side_effects=True, vmem_limit_bytes=60 * 2**20
        ),
        name="fused_block",
    )(*consts, x, table, index, cot, piece, wqkv, wproj)


def shards(latents, qkv_weight, proj_weight, merge_weight, bias_table, bias_index, cotangent):
    table = jnp.pad(bias_table, ((0, 0), (0, BUCKETS - bias_table.shape[1])))
    index = jnp.pad(bias_index, ((0, 0), (0, 2 * LANES - WINDOW)))
    cot = jnp.pad(cotangent.reshape(CELLS, OUT), ((0, SLAB - CELLS), (0, 0)))
    merged, grad, grad_table = fused(
        latents.reshape(TOKENS, WIDTH), table, index, cot, merge_weight, qkv_weight, proj_weight
    )
    return (
        merged[:CELLS].reshape(cotangent.shape),
        grad.reshape(latents.shape),
        grad_table[:, :bias_table.shape[1]],
    )


def solution(mesh):
    return jax.shard_map(
        shards,
        mesh=mesh,
        in_specs=(
            P(None, "lat", "lon", None),
            P(),
            P(),
            P("lon", None),
            P(),
            P(),
            P(None, "lat", "lon", None),
        ),
        out_specs=(P(None, "lat", "lon", None), P(None, "lat", "lon", None), P()),
        check_vma=False,
    )
```

time: 306 us -> 141 us (0.46)
  waiting for transfers between devices: 94.3 us -> 0 us
  blocking collectives: 81 us -> 0 us
  Pallas kernels: 48.7 us -> 124 us
  starting transfers between devices: 21.9 us -> 0 us
  matrix products: 20.1 us -> 0 us
  between operations: 14.6 us -> 0.67 us
  other arithmetic: 4.33 us -> 0 us
  local copies, waits for them, and re-layouts: 17.9 us -> 13.6 us
    psum x1 -> x0, blocking collectives: 81 us -> none  [shards(): grad_bias = lax.psum(grad_table[:, :bias_table.shape[1]], ('lon', 'lat'))]
    pallas_call x2 -> x1, Pallas kernels: 48.7 us -> 124 us  [fused(): pl.pallas_call(kernel, out_shape=(jax.ShapeDtypeStruct((SLAB, OUT), BF16)...]
    ppermute x8 -> x0, waiting for transfers between devices: 66.2 us -> none  [from_behind(): lax.ppermute(shard, axis, [(i, (i + by) % devices) for i in range(devices)])]
    all_gather x1 -> x0, waiting for transfers between devices: 27.4 us -> none  [shards(): weight = lax.all_gather(merge_weight, 'lon', axis=0, tiled=True)]
    ppermute x8 -> x0, starting transfers between devices: 21.9 us -> none  [from_behind(): lax.ppermute(shard, axis, [(i, (i + by) % devices) for i in range(devices)])]
    dot_general x2 -> x0, matrix products: 20.1 us -> none  [dot(): return lax.dot_general(a, b, dims, preferred_element_type=F32)]
    another operation x4 -> x0, local copies, waits for them, and re-layouts: 4.59 us -> none  [the longest x2 2.56 us: from_windows(): return shaped.reshape(level_count, lat_rows, lon_cols, features)]
    unnamed x12 -> x5, local copies, waits for them, and re-layouts: 2.6 us -> 6.17 us
  transfers between devices with their start and end apart: 9 -> 0, of which waited for: 8 -> 0; matrix products, arithmetic and copies ran while one was open for 8% -> 0% of each run, Pallas kernels for 7% -> 0%
where the time goes in v2:
time: 141 us; the launch traced here: 138 us
  Pallas kernels  124 us (88%)
  local copies, waits for them, and re-layouts  13.6 us (10%)
    pallas_call x1, Pallas kernels, fused(): pl.pallas_call(kernel, out_shape=(jax.ShapeDtypeStruct((SLAB, OUT), BF16)...  124 us
    unnamed x5, local copies, waits for them, and re-layouts  6.17 us

profile of v2, /device:TPU:1, one launch (start us, length us, event | category | flops | bytes accessed | tf_op | source)
XLA Modules:
  0.0 138.3 jit_solution(7828586262408214116)
XLA Ops:
  0.6 1.4 %pad.12.table_ref = f32[16,768]{1,0:T(8,128)} pad(f32[16,759]{1,0:T(8,128)} %param.17, f32[]{:T(128)} %constant.15.clone.1), padding=0_0x0_9 | pad | bytes 97732 | tf_op jit(solution)/shard_map/jit(_pad)/pad | solution.py:528
  2.1 1.6 %pad.13.index_ref = s32[144,256]{1,0:T(8,128)} pad(s32[144,144]{1,0:T(8,128)} %param.18, s32[]{:T(128)} %constant.16.clone.1), padding=0_0x0_112 | pad | bytes 230404 | tf_op jit(solution)/shard_map/jit(_pad)/pad | solution.py:529
  3.6 1.2 copy.21
  4.9 0.2 reshape.19
  5.1 0.8 pad.14.cot_hbm
  5.9 1.3 copy.20
  7.1 1.0 reshape.18.x_ref
  8.1 124.0 %fused_block.1 = (bf16[80,2048]{1,0:T(8,128)(2,1)}, bf16[288,1024]{1,0:T(8,128)(2,1)}, f32[16,768]{1,0:T(8,128)}) custom-call(bf16[320,288]{1,0:T(8,128)(2,1)} %constant.18.clone.nat2quad, bf16[288,320]{1,0:T(8,128)(2,1)} %constant.19.clone.quad2win, bf16[320,288]{1,0:T(8,128)(2,1)} %constant.20.clone.win2quad, bf16[288,320]{1,0:T(8,128)(2,1)} %constant.21.clone.quad2merge, ...), custom_call_target="tpu_custom_call" | custom-call | tf_op jit(solution)/shard_map/fused_block/pallas_call | solution.py:481
  132.1 1.0 slice.6
  133.1 0.2 reshape.20
  133.3 1.0 copy.22
  134.3 1.3 reshape.21
  135.6 1.3 copy.23
  136.9 1.4 %copy.25 = f32[16,759]{1,0:T(8,128)} copy(f32[16,759]{1,0:T(8,128)} %bitcast.1) | data formatting | bytes 97152

commit v3 on v2

--- a/solution.py
+++ b/solution.py
@@ -36,6 +36,10 @@
     return lax.dot_general(a, b, dims, preferred_element_type=F32)
 
 
+def lanes(start, size=LANES):
+    return pl.ds(pl.multiple_of(start, LANES), size)
+
+
 def quad_row(level, row, col):
     quad = 2 * (row // 6) + col // 3
     return quad * SLAB + level * 18 + (row % 6) * 3 + col % 3
@@ -50,11 +54,11 @@
             for col in range(6):
                 cell = (level * 12 + row) * 6 + col
                 place = quad_row(level, row, col)
-                natural[place, cell] = 1
+                natural[place, (row * 6 + col) * 4 + level] = 1
                 source = quad_row((level + 1) % 4, (row + 6) % 12, (col + 3) % 6)
                 window[cell, source] = 1
                 spot = 2 * (col % 2) + row % 2
-                merge[spot * CELLS + (level * 6 + row // 2) * 3 + col // 2, place] = 1
+                merge[spot * CELLS + (row // 2 * 3 + col // 2) * 4 + level, place] = 1
     return [jnp.asarray(m, BF16) for m in (natural, window, window.T, merge, merge.T, natural.T)]
 
 
@@ -91,7 +95,7 @@
         high = index >> 7
         found = None
         for chunk in range(BUCKETS // LANES):
-            row = table_ref[pl.ds(head, 1), chunk * LANES:(chunk + 1) * LANES]
+            row = table_ref[head, chunk:chunk + 1, :]
             spread = jnp.broadcast_to(row, (WINDOW, LANES))
             part = jnp.take_along_axis(spread, low, axis=1, mode="promise_in_bounds")
             found = part if found is None else jnp.where(high == chunk, part, found)
@@ -99,17 +103,17 @@
     return jnp.concatenate(tiles, axis=1)[:, :WINDOW]
 
 
-def attend_pair(pair, is_last, table_ref, index_ref, packed, probs_ref, attended):
-    base = pl.multiple_of(pair * LANES, LANES)
-    bias = [gather_bias(table_ref, index_ref, 2 * pair + half) for half in range(2)]
+def attend_pair(pair, is_last, biases, packed, probs_ref, attended):
+    base = pair * LANES
+    bias = [biases[2 * pair + half] for half in range(2)]
     masks = [half_mask((WINDOW, LANES), half) for half in range(2)]
     zero = jnp.zeros((WINDOW, LANES), BF16)
     for window in range(WINDOWS):
         rows = slice(window * WINDOW, (window + 1) * WINDOW)
         allowed = allowed_pairs(window, is_last)
-        query = packed[rows, pl.ds(base, LANES)] * jnp.array(HEAD_DIM ** -0.5, BF16)
-        key = packed[rows, pl.ds(WIDTH + base, LANES)]
-        value = packed[rows, pl.ds(2 * WIDTH + base, LANES)]
+        query = packed[rows, lanes(base)] * jnp.array(HEAD_DIM ** -0.5, BF16)
+        key = packed[rows, lanes(WIDTH + base)]
+        value = packed[rows, lanes(2 * WIDTH + base)]
         mixed = None
         for half in range(2):
             scores = dot(jnp.where(masks[half], query, zero), key, LAST)
@@ -119,21 +123,21 @@
             probs_ref[window, 2 * pair + half] = probs
             term = dot(probs, jnp.where(masks[half], value, zero))
             mixed = term if mixed is None else mixed + term
-        attended[rows, pl.ds(base, LANES)] = mixed.astype(BF16)
+        attended[rows, lanes(base)] = mixed.astype(BF16)
 
 
 def unattend_pair(pair, packed, probs_ref, datt, dpacked, dmain, dtail):
-    base = pl.multiple_of(pair * LANES, LANES)
+    base = pair * LANES
     scale = jnp.array(HEAD_DIM ** -0.5, BF16)
     masks = [half_mask((WINDOW, LANES), half) for half in range(2)]
     zero = jnp.zeros((WINDOW, LANES), BF16)
     sums = [None, None]
     for window in range(WINDOWS):
         rows = slice(window * WINDOW, (window + 1) * WINDOW)
-        query = packed[rows, pl.ds(base, LANES)] * scale
-        key = packed[rows, pl.ds(WIDTH + base, LANES)] * scale
-        value = packed[rows, pl.ds(2 * WIDTH + base, LANES)]
-        out_grad = datt[rows, pl.ds(base, LANES)]
+        query = packed[rows, lanes(base)] * scale
+        key = packed[rows, lanes(WIDTH + base)] * scale
+        value = packed[rows, lanes(2 * WIDTH + base)]
+        out_grad = datt[rows, lanes(base)]
         dquery, dkey, dvalue = None, None, None
         for half in range(2):
             grad = jnp.where(masks[half], out_grad, zero)
@@ -149,9 +153,9 @@
             dquery = one if dquery is None else dquery + one
             dkey = two if dkey is None else dkey + two
             dvalue = three if dvalue is None else dvalue + three
-        dpacked[rows, pl.ds(base, LANES)] = dquery.astype(BF16)
-        dpacked[rows, pl.ds(WIDTH + base, LANES)] = dkey.astype(BF16)
-        dpacked[rows, pl.ds(2 * WIDTH + base, LANES)] = dvalue.astype(BF16)
+        dpacked[rows, lanes(base)] = dquery.astype(BF16)
+        dpacked[rows, lanes(WIDTH + base)] = dkey.astype(BF16)
+        dpacked[rows, lanes(2 * WIDTH + base)] = dvalue.astype(BF16)
     for half in range(2):
         total = jnp.concatenate([sums[half], jnp.zeros((WINDOW, 2 * LANES - WINDOW), F32)], axis=1)
         for tile, store in enumerate((dmain, dtail)):
@@ -159,24 +163,44 @@
             store[pl.ds(2 * pair + half, WINDOW, stride=HEADS), :] = total[:, cols]
 
 
-def scatter_table(index_ref, dmain, dtail):
+def build_hots(index_ref, lows, hots):
+    shape = (WINDOW, WINDOW)
+    eye = lax.broadcasted_iota(jnp.int32, shape, 0) == lax.broadcasted_iota(jnp.int32, shape, 1)
+    eye = jnp.where(eye, 1.0, 0.0).astype(BF16)
+    low = (index_ref[:, :WINDOW] & (SPLIT - 1)).astype(F32).astype(BF16)
+    flipped = dot(eye, low, LAST).astype(jnp.int32)
+    lows[...] = jnp.concatenate([flipped, jnp.zeros((WINDOW, 2 * LANES - WINDOW), jnp.int32)], axis=1)
+    bucket = lax.broadcasted_iota(jnp.int32, (WINDOW, SPLIT), 1)
+
+    def build(tile):
+        def step(row, carry):
+            wanted = jnp.zeros((WINDOW, LANES), jnp.int32) + (row - tile * LANES)
+            source = lows[:, tile * LANES:(tile + 1) * LANES]
+            spread = jnp.take_along_axis(source, wanted, axis=1, mode="promise_in_bounds")
+            spread = jnp.concatenate([spread, spread], axis=1)
+            hots[row] = jnp.where(bucket == spread, 1.0, 0.0).astype(BF16)
+            return carry
+
+        return step
+
+    lax.fori_loop(0, LANES, build(0), 0, unroll=4)
+    lax.fori_loop(LANES, WINDOW, build(1), 0, unroll=4)
+
+
+def scatter_table(index_ref, hots, dmain, dtail):
     def scatter_row(row, total):
         here = pl.ds(pl.multiple_of(row * HEADS, HEADS), HEADS)
-        block = jnp.concatenate([dmain[here, :], dtail[here, :]], axis=1)
-        index = index_ref[pl.ds(row, 1), :]
-        low = index & (SPLIT - 1)
-        high = index >> 8
+        block = jnp.concatenate([dmain[here, :], dtail[here, :]], axis=1)[:, :WINDOW]
+        high = index_ref[pl.ds(row, 1), :][:, :WINDOW] >> 8
         parts = jnp.concatenate(
             [jnp.where(high == part, block, 0.0) for part in range(BUCKETS // SPLIT)], axis=0
         )
         coarse = parts.astype(BF16)
         fine = (parts - coarse.astype(F32)).astype(BF16)
-        bucket = lax.broadcasted_iota(jnp.int32, (SPLIT, 2 * LANES), 0)
-        hot = jnp.where(bucket == low, 1.0, 0.0).astype(BF16)
-        return total + dot(jnp.concatenate([coarse, fine], axis=0), hot, LAST)
+        return total + dot(jnp.concatenate([coarse, fine], axis=0), hots[row])
 
     rows = HEADS * (BUCKETS // SPLIT)
-    total = lax.fori_loop(0, WINDOW, scatter_row, jnp.zeros((2 * rows, SPLIT), F32), unroll=4)
+    total = lax.fori_loop(0, WINDOW, scatter_row, jnp.zeros((2 * rows, SPLIT), F32), unroll=8)
     total = total[:rows] + total[rows:]
     return jnp.concatenate([total[part * HEADS:(part + 1) * HEADS] for part in range(BUCKETS // SPLIT)], axis=1)
 
@@ -187,11 +211,11 @@
 
 def kernel(
     nat2quad, quad2win, win2quad, quad2merge, merge2quad, quad2nat,
-    x_ref, table_ref, index_ref, cot_hbm, piece_hbm, wqkv_hbm, wproj_hbm,
+    x_ref, table_ref, raw_index, cot_ref, piece_hbm, wqkv_hbm, wproj_hbm,
     merged_ref, grad_ref, bias_ref,
     wqkv, wproj, wbuf, cots, sent, landed, tokens, normed, packed, probs, attended,
     hats, gsend, grecv, msend, mrecv, psend, precv, datt, dpacked, dmain, dtail,
-    sum_team, sum_ring, sum_bands, local_sems, send_sems, recv_sems,
+    sum_team, sum_ring, sum_bands, chunks, index_ref, biases, lows, hots, local_sems, send_sems, recv_sems,
 ):
     lon = lax.axis_index("lon")
     lat = lax.axis_index("lat")
@@ -220,8 +244,7 @@
     loads = [
         pltpu.make_async_copy(wqkv_hbm, wqkv, local_sems.at[0]),
         pltpu.make_async_copy(wproj_hbm, wproj, local_sems.at[1]),
-        pltpu.make_async_copy(cot_hbm, cots.at[member], local_sems.at[2]),
-        pltpu.make_async_copy(piece_hbm, wbuf.at[ring], local_sems.at[3]),
+        pltpu.make_async_copy(piece_hbm, wbuf.at[ring], local_sems.at[2]),
     ]
     for load in loads:
         load.start()
@@ -258,28 +281,45 @@
     def arrived(stage, order):
         return dot(order[...], landed[stage].reshape(4 * SLAB, WIDTH))
 
-    fill(0, nat2quad, x_ref[...])
+    index_ref[...] = jnp.concatenate(
+        [raw_index[...], jnp.zeros((WINDOW, 2 * LANES - WINDOW), jnp.int32)], axis=1
+    )
+    fill(0, nat2quad, x_ref[...].astype(F32).reshape(TOKENS, WIDTH).astype(BF16))
+    cots[member] = pad_rows(cot_ref[...].astype(F32).reshape(CELLS, OUT))
     pl.semaphore_wait(barrier, len(peers))
 
     first = exchange(0, -1)
     for copy in first:
         copy.start()
 
-    half = PIECE // 2
-    ahead, behind = [], []
+    side = lax.rem(lat // 2, 2)
+    quarter = PIECE // 4
+
+    def share(part, count=1):
+        return pl.ds(pl.multiple_of(side * (2 * quarter) + part * quarter, quarter), count * quarter)
+
+    def above(step):
+        return lax.rem(ring - step + RING, RING)
+
+    def below(step):
+        return lax.rem(ring + step, RING)
+
+    ahead, behind, across = [], [], [[]]
     for step in range(4):
-        up = lax.rem(ring - step + RING, RING)
-        down = lax.rem(ring + step, RING)
         if step == 0:
-            ahead.append(remote(piece_hbm, wbuf.at[ring], ring_peer(1)))
-            behind.append(remote(piece_hbm, wbuf.at[ring], ring_peer(RING - 1)))
-        elif step < 3:
-            ahead.append(remote(wbuf.at[up], wbuf.at[up], ring_peer(1)))
-            behind.append(remote(wbuf.at[down], wbuf.at[down], ring_peer(RING - 1)))
+            ahead.append(remote(piece_hbm.at[share(0, 2)], wbuf.at[ring, share(0, 2)], ring_peer(1)))
+            behind.append(remote(piece_hbm.at[share(0, 2)], wbuf.at[ring, share(0, 2)], ring_peer(RING - 1)))
         else:
-            top, bottom = pl.ds(0, half), pl.ds(half, half)
-            ahead.append(remote(wbuf.at[up, top], wbuf.at[up, top], ring_peer(1)))
-            behind.append(remote(wbuf.at[down, bottom], wbuf.at[down, bottom], ring_peer(RING - 1)))
+            up = wbuf.at[above(step), share(0, 2 if step < 3 else 1)]
+            down = wbuf.at[below(step), share(0, 2) if step < 3 else share(1)]
+            ahead.append(remote(up, up, ring_peer(1)))
+            behind.append(remote(down, down, ring_peer(RING - 1)))
+    for step in range(1, 5):
+        moves = []
+        for spot in (above(step), below(step)) if step < 4 else (below(step),):
+            for part, peer in ((0, band_peer(2)), (1, band_peer(BANDS - 2))):
+                moves.append(remote(wbuf.at[spot, share(part)], wbuf.at[spot, share(part)], peer))
+        across.append(moves)
 
     def ring_step(step):
         if step > 0:
@@ -288,14 +328,34 @@
         if step < 4:
             ahead[step].start()
             behind[step].start()
-
-    spread = [remote(cot_hbm, cots.at[member], team_peer(step)) for step in range(1, TEAM)]
+        for copy in across[step]:
+            copy.start()
+
+    def across_wait(step):
+        for copy in across[step]:
+            copy.wait_recv()
+
+    spread = [remote(cots.at[member], cots.at[member], team_peer(step)) for step in range(1, TEAM)]
+    ring_step(0)
+
+    for chunk in range(BUCKETS // LANES):
+        cols = table_ref[:, chunk * LANES:min((chunk + 1) * LANES, table_ref.shape[1])]
+        if cols.shape[1] < LANES:
+            cols = jnp.concatenate([cols, jnp.zeros((HEADS, LANES - cols.shape[1]), F32)], axis=1)
+        for head in range(HEADS):
+            chunks[head, chunk:chunk + 1, :] = cols[head:head + 1, :]
+
+    def bias_step(head, carry):
+        biases[head] = gather_bias(chunks, index_ref, head)
+        return carry
+
+    lax.fori_loop(0, HEADS, bias_step, 0, unroll=4)
+
+    for copy in first:
+        copy.wait_recv()
     for copy in spread:
         copy.start()
-    ring_step(0)
-
-    for copy in first:
-        copy.wait_recv()
+    ring_step(1)
     values = arrived(0, quad2win)
     tokens[...] = values.astype(BF16)
     centered, inverse = stats(values)
@@ -306,12 +366,12 @@
         packed[:, cols] = dot(normed[...], wqkv[:, cols]).astype(BF16)
 
     def attend_step(pair, carry):
-        attend_pair(pair, is_last, table_ref, index_ref, packed, probs, attended)
+        attend_pair(pair, is_last, biases, packed, probs, attended)
         return carry
 
-    ring_step(1)
-    lax.fori_loop(0, PAIRS, attend_step, 0, unroll=PAIRS)
+    lax.fori_loop(0, PAIRS // 2, attend_step, 0, unroll=PAIRS // 2)
     ring_step(2)
+    lax.fori_loop(PAIRS // 2, PAIRS, attend_step, 0, unroll=PAIRS // 2)
     loads[1].wait()
     block = tokens[...].astype(F32) + dot(attended[...], wproj[...])
     fill(1, win2quad, block.astype(BF16))
@@ -322,7 +382,6 @@
     for copy in spread:
         copy.wait_recv()
     loads[2].wait()
-    loads[3].wait()
 
     def merge_grad(spot):
         rows = dot(cots[...].reshape(TEAM * SLAB, OUT), wbuf[spot], LAST).astype(BF16)
@@ -330,12 +389,16 @@
         gsend[:, :, here] = rows.reshape(TEAM, SLAB, PIECE)
 
     def merge_both(step):
-        merge_grad(lax.rem(ring - step + RING, RING))
-        merge_grad(lax.rem(ring + step, RING))
+        merge_grad(above(step))
+        merge_grad(below(step))
 
     merge_grad(ring)
+    ring_step(3)
+    across_wait(1)
     merge_both(1)
+    across_wait(2)
     merge_both(2)
+    ring_step(4)
 
     for copy in second:
         copy.wait_recv()
@@ -361,10 +424,10 @@
     for copy in inputs:
         copy.start()
 
-    ring_step(3)
+    across_wait(3)
     merge_both(3)
-    ring_step(4)
-    merge_grad(lax.rem(ring + 4, RING))
+    across_wait(4)
+    merge_grad(below(4))
     grecv[member] = gsend[member]
     grads = [
         remote(gsend.at[lax.rem(member + step, TEAM)], grecv.at[member], team_peer(step))
@@ -380,7 +443,10 @@
         rows = dot(mrecv[...].reshape(TEAM * SLAB, WIDTH), wbuf[:, :, cols].reshape(RING * PIECE, 256))
         psend[:, :, cols] = rows.astype(BF16).reshape(TEAM, SLAB, 256)
     precv[member] = psend[member]
-
+    partials = [
+        remote(psend.at[lax.rem(member + step, TEAM)], precv.at[member], team_peer(step))
+        for step in range(1, TEAM)
+    ]
     for copy in grads:
         copy.wait_recv()
     slopes = []
@@ -399,15 +465,11 @@
     third = exchange(2, -1)
     for copy in third:
         copy.start()
-    partials = [
-        remote(psend.at[lax.rem(member + step, TEAM)], precv.at[member], team_peer(step))
-        for step in range(1, TEAM)
-    ]
+    build_hots(index_ref, lows, hots)
+    for copy in third:
+        copy.wait_recv()
     for copy in partials:
         copy.start()
-
-    for copy in third:
-        copy.wait_recv()
     attended[...] = arrived(2, quad2win).astype(BF16)
     datt[...] = dot(attended[...], wproj[...], LAST).astype(BF16)
 
@@ -416,7 +478,7 @@
         return carry
 
     lax.fori_loop(0, PAIRS, unattend_step, 0, unroll=PAIRS)
-    sum_team[member] = scatter_table(index_ref, dmain, dtail)
+    sum_team[member] = scatter_table(index_ref, hots, dmain, dtail)
     team_sums = [remote(sum_team.at[member], sum_team.at[member], team_peer(step)) for step in range(1, TEAM)]
     for copy in team_sums:
         copy.start()
@@ -445,7 +507,7 @@
         total = precv[0, :, cols].astype(F32)
         for peer in range(1, TEAM):
             total = total + precv[peer, :, cols].astype(F32)
-        merged_ref[:, cols] = total.astype(BF16)
+        merged_ref[:, :, cols] = total[:CELLS].reshape(-1, 4, 256).astype(BF16)
 
     for copy in ring_sums:
         copy.wait_recv()
@@ -459,19 +521,19 @@
 
     for copy in fourth:
         copy.wait_recv()
-    grad_ref[...] = arrived(3, quad2nat).astype(BF16)
+    grad_ref[...] = arrived(3, quad2nat).reshape(-1, 4, WIDTH).astype(BF16)
 
     for copy in band_sums:
         copy.wait_recv()
     total = sum_bands[0]
     for peer in range(1, BANDS):
         total = total + sum_bands[peer]
-    bias_ref[...] = total
+    bias_ref[...] = total[:, :bias_ref.shape[1]]
     for copy in copies:
         copy.wait_send()
 
 
-COPIES = 12 + 8 + 4 * 3 + 3 + 7 + 7
+COPIES = 12 + 8 + 14 + 4 * 3 + 3 + 7 + 7
 
 
 def fused(x, table, index, cot, piece, wqkv, wproj):
@@ -481,11 +543,11 @@
     return pl.pallas_call(
         kernel,
         out_shape=(
-            jax.ShapeDtypeStruct((SLAB, OUT), BF16),
-            jax.ShapeDtypeStruct((TOKENS, WIDTH), BF16),
-            jax.ShapeDtypeStruct((HEADS, BUCKETS), F32),
+            jax.ShapeDtypeStruct(cot.shape, BF16),
+            jax.ShapeDtypeStruct(x.shape, BF16),
+            jax.ShapeDtypeStruct(table.shape, F32),
         ),
-        in_specs=[vmem] * 9 + [anywhere] * 4,
+        in_specs=[vmem] * 10 + [anywhere] * 3,
         out_specs=[vmem] * 3,
         scratch_shapes=[
             pltpu.VMEM((WIDTH, 3 * WIDTH), BF16),
@@ -513,7 +575,12 @@
             pltpu.VMEM((TEAM, HEADS, BUCKETS), F32),
             pltpu.VMEM((RING, HEADS, BUCKETS), F32),
             pltpu.VMEM((BANDS, HEADS, BUCKETS), F32),
-            pltpu.SemaphoreType.DMA((4,)),
+            pltpu.VMEM((HEADS, 8, LANES), F32),
+            pltpu.VMEM((WINDOW, 2 * LANES), jnp.int32),
+            pltpu.VMEM((HEADS, WINDOW, WINDOW), F32),
+            pltpu.VMEM((WINDOW, 2 * LANES), jnp.int32),
+            pltpu.VMEM((WINDOW, WINDOW, SPLIT), BF16),
+            pltpu.SemaphoreType.DMA((3,)),
             pltpu.SemaphoreType.DMA((COPIES,)),
             pltpu.SemaphoreType.DMA((COPIES,)),
         ],
@@ -525,16 +592,15 @@
 
 
 def shards(latents, qkv_weight, proj_weight, merge_weight, bias_table, bias_index, cotangent):
-    table = jnp.pad(bias_table, ((0, 0), (0, BUCKETS - bias_table.shape[1])))
-    index = jnp.pad(bias_index, ((0, 0), (0, 2 * LANES - WINDOW)))
-    cot = jnp.pad(cotangent.reshape(CELLS, OUT), ((0, SLAB - CELLS), (0, 0)))
+    cot = cotangent.transpose(1, 2, 0, 3)
+    cells = latents.transpose(1, 2, 0, 3)
     merged, grad, grad_table = fused(
-        latents.reshape(TOKENS, WIDTH), table, index, cot, merge_weight, qkv_weight, proj_weight
+        cells.reshape(-1, 4, WIDTH), bias_table, bias_index, cot.reshape(-1, 4, OUT), merge_weight, qkv_weight, proj_weight
     )
     return (
-        merged[:CELLS].reshape(cotangent.shape),
-        grad.reshape(latents.shape),
-        grad_table[:, :bias_table.shape[1]],
+        merged.reshape(cot.shape).transpose(2, 0, 1, 3),
+        grad.reshape(cells.shape).transpose(2, 0, 1, 3),
+        grad_table,
     )
 
 

time: 141 us -> 118 us (0.84); the launches traced: 138 us -> 118 us
  Pallas kernels: 124 us -> 112 us
  local copies, waits for them, and re-layouts: 13.6 us -> 5.35 us
    pallas_call x1, Pallas kernels: 124 us -> 112 us  [fused(): pl.pallas_call(kernel, out_shape=(jax.ShapeDtypeStruct(cot.shape, BF16),...]
    pad x3 -> x0, local copies, waits for them, and re-layouts: 3.76 us -> none  [the longest x1 1.58 us: shards(): index = jnp.pad(bias_index, ((0, 0), (0, 2 * LANES - WINDOW)))]
    reshape x4 -> x0, local copies, waits for them, and re-layouts: 2.71 us -> none  [the longest x1 1.27 us: shards(): grad.reshape(latents.shape)]
    unnamed x5 -> x3, local copies, waits for them, and re-layouts: 6.17 us -> 5.35 us
where the time goes in v3:
time: 118 us
  Pallas kernels  112 us (95%)
  local copies, waits for them, and re-layouts  5.35 us (5%)
    pallas_call x1, Pallas kernels, fused(): pl.pallas_call(kernel, out_shape=(jax.ShapeDtypeStruct(cot.shape, BF16),...  112 us
    unnamed x3, local copies, waits for them, and re-layouts  5.35 us

profile of v3, /device:TPU:1, one launch (start us, length us, event | category | flops | bytes accessed | tf_op | source)
XLA Modules:
  0.0 117.5 jit_solution(6927650341758660887)
XLA Ops:
  0.6 111.5 %fused_block.1 = (bf16[18,4,2048]{2,1,0:T(4,128)(2,1)}, bf16[72,4,1024]{2,1,0:T(4,128)(2,1)}, f32[16,759]{1,0:T(8,128)}) custom-call(bf16[320,288]{1,0:T(8,128)(2,1)} %constant.12.clone.nat2quad, bf16[288,320]{1,0:T(8,128)(2,1)} %constant.13.clone.quad2win, bf16[320,288]{1,0:T(8,128)(2,1)} %constant.14.clone.win2quad, ...), custom_call_target="tpu_custom_call" | custom-call | tf_op jit(solution)/shard_map/fused_block/pallas_call | solution.py:543
  112.2 1.8 %copy.19 = bf16[4,6,3,2048]{3,0,2,1:T(4,128)(2,1)} copy(bf16[4,6,3,2048]{3,0,2,1:T(4,128)(2,1)} %bitcast.15) | data formatting | bytes 589824
  114.0 2.1 %copy.20 = bf16[4,12,6,1024]{3,0,2,1:T(4,128)(2,1)} copy(bf16[4,12,6,1024]{3,0,2,1:T(4,128)(2,1)} %bitcast.13) | data formatting | bytes 1179648
  116.1 1.4 %copy.21 = f32[16,759]{1,0:T(8,128)} copy(f32[16,759]{1,0:T(8,128)} %get-tuple-element.14) | data formatting | bytes 97152

commit v4 on v3

--- a/solution.py
+++ b/solution.py
@@ -25,6 +25,7 @@
 PIECE = 128
 CELLS = 72
 SLAB = 80
+HALF = 40
 F32 = jnp.float32
 BF16 = jnp.bfloat16
 LAST = (((1,), (1,)), ((), ()))
@@ -41,14 +42,15 @@
 
 
 def quad_row(level, row, col):
+    window, inner = divmod((level + 3) % 4, 2)
     quad = 2 * (row // 6) + col // 3
-    return quad * SLAB + level * 18 + (row % 6) * 3 + col % 3
+    return window * 4 * HALF + quad * HALF + inner * 18 + (row % 6) * 3 + col % 3
 
 
 def orders():
-    natural = np.zeros((4 * SLAB, TOKENS), np.float32)
-    window = np.zeros((TOKENS, 4 * SLAB), np.float32)
-    merge = np.zeros((TOKENS, 4 * SLAB), np.float32)
+    natural = np.zeros((8 * HALF, TOKENS), np.float32)
+    window = np.zeros((TOKENS, 8 * HALF), np.float32)
+    merge = np.zeros((TOKENS, 8 * HALF), np.float32)
     for level in range(4):
         for row in range(12):
             for col in range(6):
@@ -59,6 +61,7 @@
                 window[cell, source] = 1
                 spot = 2 * (col % 2) + row % 2
                 merge[spot * CELLS + (row // 2 * 3 + col // 2) * 4 + level, place] = 1
+    window = window[:WINDOW, :4 * HALF]
     return [jnp.asarray(m, BF16) for m in (natural, window, window.T, merge, merge.T, natural.T)]
 
 
@@ -103,64 +106,63 @@
     return jnp.concatenate(tiles, axis=1)[:, :WINDOW]
 
 
-def attend_pair(pair, is_last, biases, packed, probs_ref, attended):
+def attend_pair(pair, window, is_last, biases, packed, probs_ref, attended):
     base = pair * LANES
     bias = [biases[2 * pair + half] for half in range(2)]
     masks = [half_mask((WINDOW, LANES), half) for half in range(2)]
     zero = jnp.zeros((WINDOW, LANES), BF16)
-    for window in range(WINDOWS):
-        rows = slice(window * WINDOW, (window + 1) * WINDOW)
-        allowed = allowed_pairs(window, is_last)
-        query = packed[rows, lanes(base)] * jnp.array(HEAD_DIM ** -0.5, BF16)
-        key = packed[rows, lanes(WIDTH + base)]
-        value = packed[rows, lanes(2 * WIDTH + base)]
-        mixed = None
-        for half in range(2):
-            scores = dot(jnp.where(masks[half], query, zero), key, LAST)
-            scores = jnp.where(allowed, scores + bias[half], MASKED)
-            weights = jnp.exp(scores - jnp.max(scores, axis=-1, keepdims=True))
-            probs = (weights * (1.0 / jnp.sum(weights, axis=-1, keepdims=True))).astype(BF16)
-            probs_ref[window, 2 * pair + half] = probs
-            term = dot(probs, jnp.where(masks[half], value, zero))
-            mixed = term if mixed is None else mixed + term
-        attended[rows, lanes(base)] = mixed.astype(BF16)
-
-
-def unattend_pair(pair, packed, probs_ref, datt, dpacked, dmain, dtail):
+    rows = slice(window * WINDOW, (window + 1) * WINDOW)
+    allowed = allowed_pairs(window, is_last)
+    query = packed[rows, lanes(base)] * jnp.array(HEAD_DIM ** -0.5, BF16)
+    key = packed[rows, lanes(WIDTH + base)]
+    value = packed[rows, lanes(2 * WIDTH + base)]
+    mixed = None
+    for half in range(2):
+        scores = dot(jnp.where(masks[half], query, zero), key, LAST)
+        scores = jnp.where(allowed, scores + bias[half], MASKED)
+        weights = jnp.exp(scores - jnp.max(scores, axis=-1, keepdims=True))
+        probs = (weights * (1.0 / jnp.sum(weights, axis=-1, keepdims=True))).astype(BF16)
+        probs_ref[window, 2 * pair + half] = probs
+        term = dot(probs, jnp.where(masks[half], value, zero))
+        mixed = term if mixed is None else mixed + term
+    attended[rows, lanes(base)] = mixed.astype(BF16)
+
+
+def unattend_pair(pair, window, packed, probs_ref, datt, dpacked, dmain, dtail):
     base = pair * LANES
     scale = jnp.array(HEAD_DIM ** -0.5, BF16)
     masks = [half_mask((WINDOW, LANES), half) for half in range(2)]
     zero = jnp.zeros((WINDOW, LANES), BF16)
     sums = [None, None]
-    for window in range(WINDOWS):
-        rows = slice(window * WINDOW, (window + 1) * WINDOW)
-        query = packed[rows, lanes(base)] * scale
-        key = packed[rows, lanes(WIDTH + base)] * scale
-        value = packed[rows, lanes(2 * WIDTH + base)]
-        out_grad = datt[rows, lanes(base)]
-        dquery, dkey, dvalue = None, None, None
-        for half in range(2):
-            grad = jnp.where(masks[half], out_grad, zero)
-            probs = probs_ref[window, 2 * pair + half]
-            wide = probs.astype(F32)
-            product = wide * dot(grad, value, LAST)
-            ds = product - wide * jnp.sum(product, axis=-1, keepdims=True)
-            sums[half] = ds if sums[half] is None else sums[half] + ds
-            narrow = ds.astype(BF16)
-            one = dot(narrow, jnp.where(masks[half], key, zero))
-            two = dot(narrow, jnp.where(masks[half], query, zero), FIRST)
-            three = dot(probs, grad, FIRST)
-            dquery = one if dquery is None else dquery + one
-            dkey = two if dkey is None else dkey + two
-            dvalue = three if dvalue is None else dvalue + three
-        dpacked[rows, lanes(base)] = dquery.astype(BF16)
-        dpacked[rows, lanes(WIDTH + base)] = dkey.astype(BF16)
-        dpacked[rows, lanes(2 * WIDTH + base)] = dvalue.astype(BF16)
+    rows = slice(window * WINDOW, (window + 1) * WINDOW)
+    query = packed[rows, lanes(base)] * scale
+    key = packed[rows, lanes(WIDTH + base)] * scale
+    value = packed[rows, lanes(2 * WIDTH + base)]
+    out_grad = datt[rows, lanes(base)]
+    dquery, dkey, dvalue = None, None, None
+    for half in range(2):
+        grad = jnp.where(masks[half], out_grad, zero)
+        probs = probs_ref[window, 2 * pair + half]
+        wide = probs.astype(F32)
+        product = wide * dot(grad, value, LAST)
+        ds = product - wide * jnp.sum(product, axis=-1, keepdims=True)
+        sums[half] = ds
+        narrow = ds.astype(BF16)
+        one = dot(narrow, jnp.where(masks[half], key, zero))
+        two = dot(narrow, jnp.where(masks[half], query, zero), FIRST)
+        three = dot(probs, grad, FIRST)
+        dquery = one if dquery is None else dquery + one
+        dkey = two if dkey is None else dkey + two
+        dvalue = three if dvalue is None else dvalue + three
+    dpacked[rows, lanes(base)] = dquery.astype(BF16)
+    dpacked[rows, lanes(WIDTH + base)] = dkey.astype(BF16)
+    dpacked[rows, lanes(2 * WIDTH + base)] = dvalue.astype(BF16)
     for half in range(2):
         total = jnp.concatenate([sums[half], jnp.zeros((WINDOW, 2 * LANES - WINDOW), F32)], axis=1)
         for tile, store in enumerate((dmain, dtail)):
             cols = slice(tile * LANES, (tile + 1) * LANES)
-            store[pl.ds(2 * pair + half, WINDOW, stride=HEADS), :] = total[:, cols]
+            here = pl.ds(2 * pair + half, WINDOW, stride=HEADS)
+            store[here, :] = total[:, cols] if window == 0 else store[here, :] + total[:, cols]
 
 
 def build_hots(index_ref, lows, hots):
@@ -266,30 +268,50 @@
 
     def exchange(stage, side):
         moves = []
-        for quad, (rows, cols) in enumerate(((1, 1), (1, 0), (0, 1))):
-            moves.append(remote(sent.at[stage, quad], landed.at[stage, quad], near(side * rows, side * cols)))
+        for window in range(WINDOWS):
+            moves.append([])
+            for quad, (rows, cols) in enumerate(((1, 1), (1, 0), (0, 1))):
+                source, target = sent.at[stage, window, quad], landed.at[stage, window, quad]
+                moves[-1].append(remote(source, target, near(side * rows, side * cols)))
         return moves
 
-    def fill(stage, order, values):
+    def fill(stage, window, order, values):
+        rows = dot(order, values)
         for quad in range(4):
-            rows = dot(order[quad * SLAB:(quad + 1) * SLAB, :], values).astype(BF16)
+            part = rows[quad * HALF:(quad + 1) * HALF]
+            part = jnp.concatenate([part[:, :WIDTH // 2], part[:, WIDTH // 2:]], axis=0).astype(BF16)
             if quad == 3:
-                landed[stage, quad] = rows
+                landed[stage, window, quad] = part
             else:
-                sent[stage, quad] = rows
-
-    def arrived(stage, order):
-        return dot(order[...], landed[stage].reshape(4 * SLAB, WIDTH))
+                sent[stage, window, quad] = part
+
+    def fill_both(stage, order, values):
+        for window in range(WINDOWS):
+            fill(stage, window, order[window * 4 * HALF:(window + 1) * 4 * HALF, :], values)
+
+    def halves(stage, window):
+        block = landed[stage, window].astype(F32)
+        rows = jnp.concatenate([block[:, :HALF], block[:, HALF:]], axis=2)
+        return rows.reshape(4 * HALF, WIDTH).astype(BF16)
+
+    def arrived(stage, window):
+        return dot(quad2win[...], halves(stage, window))
+
+    def arrived_both(stage, order):
+        return dot(order[...], jnp.concatenate([halves(stage, window) for window in range(WINDOWS)], axis=0))
+
+    def span(window):
+        return slice(window * WINDOW, (window + 1) * WINDOW)
 
     index_ref[...] = jnp.concatenate(
         [raw_index[...], jnp.zeros((WINDOW, 2 * LANES - WINDOW), jnp.int32)], axis=1
     )
-    fill(0, nat2quad, x_ref[...].astype(F32).reshape(TOKENS, WIDTH).astype(BF16))
+    fill_both(0, nat2quad, x_ref[...].astype(F32).reshape(TOKENS, WIDTH).astype(BF16))
     cots[member] = pad_rows(cot_ref[...].astype(F32).reshape(CELLS, OUT))
     pl.semaphore_wait(barrier, len(peers))
 
     first = exchange(0, -1)
-    for copy in first:
+    for copy in first[0] + first[1]:
         copy.start()
 
     side = lax.rem(lat // 2, 2)
@@ -351,33 +373,39 @@
 
     lax.fori_loop(0, HEADS, bias_step, 0, unroll=4)
 
-    for copy in first:
+    for copy in first[0] + first[1]:
         copy.wait_recv()
     for copy in spread:
         copy.start()
     ring_step(1)
-    values = arrived(0, quad2win)
-    tokens[...] = values.astype(BF16)
-    centered, inverse = stats(values)
-    normed[...] = (centered * inverse).astype(BF16)
+    for window in range(WINDOWS):
+        values = arrived(0, window)
+        tokens[span(window), :] = values.astype(BF16)
+        centered, inverse = stats(values)
+        normed[span(window), :] = (centered * inverse).astype(BF16)
     loads[0].wait()
     for part in range(12):
         cols = slice(part * 256, (part + 1) * 256)
         packed[:, cols] = dot(normed[...], wqkv[:, cols]).astype(BF16)
 
-    def attend_step(pair, carry):
-        attend_pair(pair, is_last, biases, packed, probs, attended)
-        return carry
-
-    lax.fori_loop(0, PAIRS // 2, attend_step, 0, unroll=PAIRS // 2)
-    ring_step(2)
-    lax.fori_loop(PAIRS // 2, PAIRS, attend_step, 0, unroll=PAIRS // 2)
+    def attend_step(window):
+        def step(pair, carry):
+            attend_pair(pair, window, is_last, biases, packed, probs, attended)
+            return carry
+
+        return step
+
+    second = exchange(1, 1)
     loads[1].wait()
-    block = tokens[...].astype(F32) + dot(attended[...], wproj[...])
-    fill(1, win2quad, block.astype(BF16))
-    second = exchange(1, 1)
-    for copy in second:
-        copy.start()
+    for window in range(WINDOWS):
+        lax.fori_loop(0, PAIRS, attend_step(window), 0, unroll=PAIRS)
+        rows = span(window)
+        block = tokens[rows, :].astype(F32) + dot(attended[rows, :], wproj[...])
+        fill(1, window, win2quad[...], block.astype(BF16))
+        for copy in second[window]:
+            copy.start()
+        if window == 0:
+            ring_step(2)
 
     for copy in spread:
         copy.wait_recv()
@@ -400,9 +428,9 @@
     merge_both(2)
     ring_step(4)
 
-    for copy in second:
-        copy.wait_recv()
-    slabs = arrived(1, quad2merge)
+    for copy in second[0] + second[1]:
+        copy.wait_recv()
+    slabs = arrived_both(1, quad2merge)
     parts = [slabs[spot * CELLS:(spot + 1) * CELLS] for spot in range(4)]
     total = sum(jnp.sum(part, axis=-1, keepdims=True) for part in parts)
     average = total * (1.0 / (4 * WIDTH))
@@ -461,37 +489,50 @@
         jnp.sum(s * hats[spot], axis=-1, keepdims=True) for spot, s in enumerate(slopes)
     ) * (1.0 / (4 * WIDTH))
     slopes = [merge_inverse * (s - mean_slope - hats[spot] * mean_tilt) for spot, s in enumerate(slopes)]
-    fill(2, merge2quad, jnp.concatenate(slopes, axis=0).astype(BF16))
+    fill_both(2, merge2quad, jnp.concatenate(slopes, axis=0).astype(BF16))
     third = exchange(2, -1)
-    for copy in third:
+    for copy in third[0] + third[1]:
         copy.start()
     build_hots(index_ref, lows, hots)
-    for copy in third:
-        copy.wait_recv()
+
+    def unattend_step(window):
+        def step(pair, carry):
+            unattend_pair(pair, window, packed, probs, datt, dpacked, dmain, dtail)
+            return carry
+
+        return step
+
+    def unattend(window):
+        for copy in third[window]:
+            copy.wait_recv()
+        rows = span(window)
+        attended[rows, :] = arrived(2, window).astype(BF16)
+        datt[rows, :] = dot(attended[rows, :], wproj[...], LAST).astype(BF16)
+        lax.fori_loop(0, PAIRS, unattend_step(window), 0, unroll=PAIRS)
+
+    fourth = exchange(3, 1)
+
+    def finish(window):
+        rows = span(window)
+        dnormed = dot(dpacked[rows, :], wqkv[...], LAST).astype(BF16).astype(F32)
+        centered, inverse = stats(tokens[rows, :].astype(F32))
+        hat = centered * inverse
+        slope = jnp.mean(dnormed * hat, axis=-1, keepdims=True)
+        inner = inverse * (dnormed - jnp.mean(dnormed, axis=-1, keepdims=True) - hat * slope)
+        fill(3, window, win2quad[...], (attended[rows, :].astype(F32) + inner).astype(BF16))
+        for copy in fourth[window]:
+            copy.start()
+
+    unattend(0)
+    finish(0)
     for copy in partials:
         copy.start()
-    attended[...] = arrived(2, quad2win).astype(BF16)
-    datt[...] = dot(attended[...], wproj[...], LAST).astype(BF16)
-
-    def unattend_step(pair, carry):
-        unattend_pair(pair, packed, probs, datt, dpacked, dmain, dtail)
-        return carry
-
-    lax.fori_loop(0, PAIRS, unattend_step, 0, unroll=PAIRS)
+    unattend(1)
     sum_team[member] = scatter_table(index_ref, hots, dmain, dtail)
     team_sums = [remote(sum_team.at[member], sum_team.at[member], team_peer(step)) for step in range(1, TEAM)]
     for copy in team_sums:
         copy.start()
-
-    dnormed = dot(dpacked[...], wqkv[...], LAST).astype(BF16).astype(F32)
-    centered, inverse = stats(tokens[...].astype(F32))
-    hat = centered * inverse
-    slope = jnp.mean(dnormed * hat, axis=-1, keepdims=True)
-    inner = inverse * (dnormed - jnp.mean(dnormed, axis=-1, keepdims=True) - hat * slope)
-    fill(3, win2quad, (attended[...].astype(F32) + inner).astype(BF16))
-    fourth = exchange(3, 1)
-    for copy in fourth:
-        copy.start()
+    finish(1)
 
     for copy in team_sums:
         copy.wait_recv()
@@ -507,7 +548,7 @@
         total = precv[0, :, cols].astype(F32)
         for peer in range(1, TEAM):
             total = total + precv[peer, :, cols].astype(F32)
-        merged_ref[:, :, cols] = total[:CELLS].reshape(-1, 4, 256).astype(BF16)
+        merged_ref[:, cols] = total[:CELLS].astype(BF16)
 
     for copy in ring_sums:
         copy.wait_recv()
@@ -519,9 +560,9 @@
     for copy in band_sums:
         copy.start()
 
-    for copy in fourth:
-        copy.wait_recv()
-    grad_ref[...] = arrived(3, quad2nat).reshape(-1, 4, WIDTH).astype(BF16)
+    for copy in fourth[0] + fourth[1]:
+        copy.wait_recv()
+    grad_ref[...] = arrived_both(3, quad2nat).astype(BF16)
 
     for copy in band_sums:
         copy.wait_recv()
@@ -533,7 +574,7 @@
         copy.wait_send()
 
 
-COPIES = 12 + 8 + 14 + 4 * 3 + 3 + 7 + 7
+COPIES = 24 + 8 + 14 + 4 * 3 + 3 + 7 + 7
 
 
 def fused(x, table, index, cot, piece, wqkv, wproj):
@@ -543,8 +584,8 @@
     return pl.pallas_call(
         kernel,
         out_shape=(
-            jax.ShapeDtypeStruct(cot.shape, BF16),
-            jax.ShapeDtypeStruct(x.shape, BF16),
+            jax.ShapeDtypeStruct((CELLS, OUT), BF16),
+            jax.ShapeDtypeStruct((TOKENS, WIDTH), BF16),
             jax.ShapeDtypeStruct(table.shape, F32),
         ),
         in_specs=[vmem] * 10 + [anywhere] * 3,
@@ -554,8 +595,8 @@
             pltpu.VMEM((WIDTH, WIDTH), BF16),
             pltpu.VMEM((RING, PIECE, OUT), BF16),
             pltpu.VMEM((TEAM, SLAB, OUT), BF16),
-            pltpu.VMEM((4, 3, SLAB, WIDTH), BF16),
-            pltpu.VMEM((4, 4, SLAB, WIDTH), BF16),
+            pltpu.VMEM((4, WINDOWS, 3, 2 * HALF, WIDTH // 2), BF16),
+            pltpu.VMEM((4, WINDOWS, 4, 2 * HALF, WIDTH // 2), BF16),
             pltpu.VMEM((TOKENS, WIDTH), BF16),
             pltpu.VMEM((TOKENS, WIDTH), BF16),
             pltpu.VMEM((TOKENS, 3 * WIDTH), BF16),

time: 118 us -> 126 us (1.068)
  Pallas kernels: 112 us -> 120 us
    pallas_call x1, Pallas kernels: 112 us -> 120 us  [fused(): pl.pallas_call(kernel, out_shape=(jax.ShapeDtypeStruct((CELLS, OUT), BF16...]
    reshape x0 -> x2, local copies, waits for them, and re-layouts: none -> 4.03 us  [the longest x1 2.24 us: shards(): grad.reshape(cells.shape).transpose(2, 0, 1, 3)]
    unnamed x3 -> x1, local copies, waits for them, and re-layouts: 5.35 us -> 1.42 us
where the time goes in v4:
time: 126 us
  Pallas kernels  120 us (95%)
  local copies, waits for them, and re-layouts  5.45 us (4%)
    pallas_call x1, Pallas kernels, fused(): pl.pallas_call(kernel, out_shape=(jax.ShapeDtypeStruct((CELLS, OUT), BF16...  120 us

profile of v4, /device:TPU:1, one launch (start us, length us, event | category | flops | bytes accessed | tf_op | source)
XLA Modules:
  0.0 125.9 jit_solution(16219282132867768834)
XLA Ops:
  0.6 119.8 %fused_block.1 = (bf16[72,2048]{1,0:T(8,128)(2,1)}, bf16[288,1024]{1,0:T(8,128)(2,1)}, f32[16,759]{1,0:T(8,128)}) custom-call(bf16[320,288]{1,0:T(8,128)(2,1)} %constant.12.clone.nat2quad, bf16[144,160]{1,0:T(8,128)(2,1)} %constant.13.clone.quad2win, bf16[160,144]{1,0:T(8,128)(2,1)} %constant.14.clone.win2quad, bf16[288,320]{1,0:T(8,128)(2,1)} %constant.15.clone.quad2merge, ...), custom_call_target="tpu_custom_call" | custom-call | tf_op jit(solution)/shard_map/fused_block/pallas_call | solution.py:584
  120.4 1.8 %reshape.20 = bf16[6,3,4,2048]{3,2,1,0:T(4,128)(2,1)} reshape(bf16[72,2048]{1,0:T(8,128)(2,1)} %get-tuple-element.6) | data formatting | bytes 589824 | tf_op jit(solution)/shard_map/reshape | solution.py:642
  122.2 2.2 %reshape.21 = bf16[12,6,4,1024]{3,2,1,0:T(4,128)(2,1)} reshape(bf16[288,1024]{1,0:T(8,128)(2,1)} %get-tuple-element.7) | data formatting | bytes 1179648 | tf_op jit(solution)/shard_map/reshape | solution.py:643
  124.5 1.4 %copy.17 = f32[16,759]{1,0:T(8,128)} copy(f32[16,759]{1,0:T(8,128)} %get-tuple-element.14) | data formatting | bytes 97152

commit v5 on v3

--- a/solution.py
+++ b/solution.py
@@ -42,13 +42,13 @@
 
 def quad_row(level, row, col):
     quad = 2 * (row // 6) + col // 3
-    return quad * SLAB + level * 18 + (row % 6) * 3 + col % 3
+    return quad * CELLS + level * 18 + (row % 6) * 3 + col % 3
 
 
 def orders():
-    natural = np.zeros((4 * SLAB, TOKENS), np.float32)
-    window = np.zeros((TOKENS, 4 * SLAB), np.float32)
-    merge = np.zeros((TOKENS, 4 * SLAB), np.float32)
+    natural = np.zeros((TOKENS, TOKENS), np.float32)
+    window = np.zeros((TOKENS, TOKENS), np.float32)
+    merge = np.zeros((TOKENS, TOKENS), np.float32)
     for level in range(4):
         for row in range(12):
             for col in range(6):
@@ -271,15 +271,19 @@
         return moves
 
     def fill(stage, order, values):
+        rows = dot(order[...], values)
         for quad in range(4):
-            rows = dot(order[quad * SLAB:(quad + 1) * SLAB, :], values).astype(BF16)
+            part = rows[quad * CELLS:(quad + 1) * CELLS]
+            part = jnp.concatenate([part[:, :WIDTH // 2], part[:, WIDTH // 2:]], axis=0).astype(BF16)
             if quad == 3:
-                landed[stage, quad] = rows
+                landed[stage, quad] = part
             else:
-                sent[stage, quad] = rows
+                sent[stage, quad] = part
 
     def arrived(stage, order):
-        return dot(order[...], landed[stage].reshape(4 * SLAB, WIDTH))
+        block = landed[stage].astype(F32)
+        rows = jnp.concatenate([block[:, :CELLS], block[:, CELLS:]], axis=2)
+        return dot(order[...], rows.reshape(TOKENS, WIDTH).astype(BF16))
 
     index_ref[...] = jnp.concatenate(
         [raw_index[...], jnp.zeros((WINDOW, 2 * LANES - WINDOW), jnp.int32)], axis=1
@@ -442,11 +446,16 @@
         cols = slice(part * 256, (part + 1) * 256)
         rows = dot(mrecv[...].reshape(TEAM * SLAB, WIDTH), wbuf[:, :, cols].reshape(RING * PIECE, 256))
         psend[:, :, cols] = rows.astype(BF16).reshape(TEAM, SLAB, 256)
-    precv[member] = psend[member]
+    core = lax.rem(member, 2)
+    home = member - core
+    sibling = {"lon": ring * TEAM + home + 1 - core, "lat": lat}
+    other = {"lon": ring * TEAM + 2 - home + core, "lat": lat}
     partials = [
-        remote(psend.at[lax.rem(member + step, TEAM)], precv.at[member], team_peer(step))
-        for step in range(1, TEAM)
+        remote(psend.at[home + 1 - core], precv.at[0], sibling),
+        remote(psend.at[2 - home + 1 - core], precv.at[1], sibling),
     ]
+    for copy in partials:
+        copy.start()
     for copy in grads:
         copy.wait_recv()
     slopes = []
@@ -469,7 +478,10 @@
     for copy in third:
         copy.wait_recv()
     for copy in partials:
-        copy.start()
+        copy.wait_recv()
+    precv[3] = (psend[2 - home + core].astype(F32) + precv[1].astype(F32)).astype(BF16)
+    summed = remote(precv.at[3], precv.at[2], other)
+    summed.start()
     attended[...] = arrived(2, quad2win).astype(BF16)
     datt[...] = dot(attended[...], wproj[...], LAST).astype(BF16)
 
@@ -478,11 +490,6 @@
         return carry
 
     lax.fori_loop(0, PAIRS, unattend_step, 0, unroll=PAIRS)
-    sum_team[member] = scatter_table(index_ref, hots, dmain, dtail)
-    team_sums = [remote(sum_team.at[member], sum_team.at[member], team_peer(step)) for step in range(1, TEAM)]
-    for copy in team_sums:
-        copy.start()
-
     dnormed = dot(dpacked[...], wqkv[...], LAST).astype(BF16).astype(F32)
     centered, inverse = stats(tokens[...].astype(F32))
     hat = centered * inverse
@@ -493,6 +500,19 @@
     for copy in fourth:
         copy.start()
 
+    sum_team[member] = scatter_table(index_ref, hots, dmain, dtail)
+    team_sums = [remote(sum_team.at[member], sum_team.at[member], team_peer(step)) for step in range(1, TEAM)]
+    for copy in team_sums:
+        copy.start()
+
+    summed.wait_recv()
+    for part in range(8):
+        cols = slice(part * 256, (part + 1) * 256)
+        total = psend[member, :, cols].astype(F32)
+        for peer in (0, 2):
+            total = total + precv[peer, :, cols].astype(F32)
+        merged_ref[:, :, cols] = total[:CELLS].reshape(-1, 4, 256).astype(BF16)
+
     for copy in team_sums:
         copy.wait_recv()
     sum_ring[ring] = sum_team[0] + sum_team[1] + sum_team[2] + sum_team[3]
@@ -500,14 +520,9 @@
     for copy in ring_sums:
         copy.start()
 
-    for copy in partials:
-        copy.wait_recv()
-    for part in range(8):
-        cols = slice(part * 256, (part + 1) * 256)
-        total = precv[0, :, cols].astype(F32)
-        for peer in range(1, TEAM):
-            total = total + precv[peer, :, cols].astype(F32)
-        merged_ref[:, :, cols] = total[:CELLS].reshape(-1, 4, 256).astype(BF16)
+    for copy in fourth:
+        copy.wait_recv()
+    grad_ref[...] = arrived(3, quad2nat).reshape(-1, 4, WIDTH).astype(BF16)
 
     for copy in ring_sums:
         copy.wait_recv()
@@ -518,10 +533,6 @@
     band_sums = [remote(sum_bands.at[lat], sum_bands.at[lat], band_peer(step)) for step in range(1, BANDS)]
     for copy in band_sums:
         copy.start()
-
-    for copy in fourth:
-        copy.wait_recv()
-    grad_ref[...] = arrived(3, quad2nat).reshape(-1, 4, WIDTH).astype(BF16)
 
     for copy in band_sums:
         copy.wait_recv()
@@ -554,8 +565,8 @@
             pltpu.VMEM((WIDTH, WIDTH), BF16),
             pltpu.VMEM((RING, PIECE, OUT), BF16),
             pltpu.VMEM((TEAM, SLAB, OUT), BF16),
-            pltpu.VMEM((4, 3, SLAB, WIDTH), BF16),
-            pltpu.VMEM((4, 4, SLAB, WIDTH), BF16),
+            pltpu.VMEM((4, 3, 2 * CELLS, WIDTH // 2), BF16),
+            pltpu.VMEM((4, 4, 2 * CELLS, WIDTH // 2), BF16),
             pltpu.VMEM((TOKENS, WIDTH), BF16),
             pltpu.VMEM((TOKENS, WIDTH), BF16),
             pltpu.VMEM((TOKENS, 3 * WIDTH), BF16),

time: 118 us -> 119 us (level)
  no operation moved by 1% of the time
where the time goes in v5:
time: 119 us; the launch traced here: 118 us
  Pallas kernels  112 us (94%)
  local copies, waits for them, and re-layouts  5.35 us (4%)
    pallas_call x1, Pallas kernels, fused(): pl.pallas_call(kernel, out_shape=(jax.ShapeDtypeStruct(cot.shape, BF16),...  112 us
    unnamed x3, local copies, waits for them, and re-layouts  5.35 us

profile of v5, /device:TPU:1, one launch (start us, length us, event | category | flops | bytes accessed | tf_op | source)
XLA Modules:
  0.0 118.3 jit_solution(5187642676956778333)
XLA Ops:
  0.6 112.4 %fused_block.1 = (bf16[18,4,2048]{2,1,0:T(4,128)(2,1)}, bf16[72,4,1024]{2,1,0:T(4,128)(2,1)}, f32[16,759]{1,0:T(8,128)}) custom-call(bf16[288,288]{1,0:T(8,128)(2,1)} %constant.12.clone.nat2quad, bf16[288,288]{1,0:T(8,128)(2,1)} %constant.13.clone.quad2win, bf16[288,288]{1,0:T(8,128)(2,1)} %constant.14.clone.win2quad, ...), custom_call_target="tpu_custom_call" | custom-call | tf_op jit(solution)/shard_map/fused_block/pallas_call | solution.py:554
  113.0 1.8 %copy.19 = bf16[4,6,3,2048]{3,0,2,1:T(4,128)(2,1)} copy(bf16[4,6,3,2048]{3,0,2,1:T(4,128)(2,1)} %bitcast.15) | data formatting | bytes 589824
  114.8 2.1 %copy.20 = bf16[4,12,6,1024]{3,0,2,1:T(4,128)(2,1)} copy(bf16[4,12,6,1024]{3,0,2,1:T(4,128)(2,1)} %bitcast.13) | data formatting | bytes 1179648
  116.9 1.4 %copy.21 = f32[16,759]{1,0:T(8,128)} copy(f32[16,759]{1,0:T(8,128)} %get-tuple-element.14) | data formatting | bytes 97152

commit v6 on v5

--- a/solution.py
+++ b/solution.py
@@ -42,13 +42,13 @@
 
 def quad_row(level, row, col):
     quad = 2 * (row // 6) + col // 3
-    return quad * CELLS + level * 18 + (row % 6) * 3 + col % 3
+    return quad * SLAB + level * 18 + (row % 6) * 3 + col % 3
 
 
 def orders():
-    natural = np.zeros((TOKENS, TOKENS), np.float32)
-    window = np.zeros((TOKENS, TOKENS), np.float32)
-    merge = np.zeros((TOKENS, TOKENS), np.float32)
+    natural = np.zeros((4 * SLAB, TOKENS), np.float32)
+    window = np.zeros((TOKENS, 4 * SLAB), np.float32)
+    merge = np.zeros((TOKENS, 4 * SLAB), np.float32)
     for level in range(4):
         for row in range(12):
             for col in range(6):
@@ -271,19 +271,15 @@
         return moves
 
     def fill(stage, order, values):
-        rows = dot(order[...], values)
         for quad in range(4):
-            part = rows[quad * CELLS:(quad + 1) * CELLS]
-            part = jnp.concatenate([part[:, :WIDTH // 2], part[:, WIDTH // 2:]], axis=0).astype(BF16)
+            rows = dot(order[quad * SLAB:(quad + 1) * SLAB, :], values).astype(BF16)
             if quad == 3:
-                landed[stage, quad] = part
+                landed[stage, quad] = rows
             else:
-                sent[stage, quad] = part
+                sent[stage, quad] = rows
 
     def arrived(stage, order):
-        block = landed[stage].astype(F32)
-        rows = jnp.concatenate([block[:, :CELLS], block[:, CELLS:]], axis=2)
-        return dot(order[...], rows.reshape(TOKENS, WIDTH).astype(BF16))
+        return dot(order[...], landed[stage].reshape(4 * SLAB, WIDTH))
 
     index_ref[...] = jnp.concatenate(
         [raw_index[...], jnp.zeros((WINDOW, 2 * LANES - WINDOW), jnp.int32)], axis=1
@@ -565,8 +561,8 @@
             pltpu.VMEM((WIDTH, WIDTH), BF16),
             pltpu.VMEM((RING, PIECE, OUT), BF16),
             pltpu.VMEM((TEAM, SLAB, OUT), BF16),
-            pltpu.VMEM((4, 3, 2 * CELLS, WIDTH // 2), BF16),
-            pltpu.VMEM((4, 4, 2 * CELLS, WIDTH // 2), BF16),
+            pltpu.VMEM((4, 3, SLAB, WIDTH), BF16),
+            pltpu.VMEM((4, 4, SLAB, WIDTH), BF16),
             pltpu.VMEM((TOKENS, WIDTH), BF16),
             pltpu.VMEM((TOKENS, WIDTH), BF16),
             pltpu.VMEM((TOKENS, 3 * WIDTH), BF16),

time: 119 us -> 122 us (1.025)
  Pallas kernels: 112 us -> 115 us
    pallas_call x1, Pallas kernels: 112 us -> 115 us  [fused(): pl.pallas_call(kernel, out_shape=(jax.ShapeDtypeStruct(cot.shape, BF16),...]
where the time goes in v6:
time: 122 us; the launch traced here: 121 us
  Pallas kernels  115 us (94%)
  local copies, waits for them, and re-layouts  5.35 us (4%)
    pallas_call x1, Pallas kernels, fused(): pl.pallas_call(kernel, out_shape=(jax.ShapeDtypeStruct(cot.shape, BF16),...  115 us
    unnamed x3, local copies, waits for them, and re-layouts  5.35 us

profile of v6, /device:TPU:1, one launch (start us, length us, event | category | flops | bytes accessed | tf_op | source)
XLA Modules:
  0.0 121.1 jit_solution(558432821932614297)
XLA Ops:
  0.6 115.1 %fused_block.1 = (bf16[18,4,2048]{2,1,0:T(4,128)(2,1)}, bf16[72,4,1024]{2,1,0:T(4,128)(2,1)}, f32[16,759]{1,0:T(8,128)}) custom-call(bf16[320,288]{1,0:T(8,128)(2,1)} %constant.12.clone.nat2quad, bf16[288,320]{1,0:T(8,128)(2,1)} %constant.13.clone.quad2win, bf16[320,288]{1,0:T(8,128)(2,1)} %constant.14.clone.win2quad, ...), custom_call_target="tpu_custom_call" | custom-call | tf_op jit(solution)/shard_map/fused_block/pallas_call | solution.py:550
  115.8 1.8 %copy.19 = bf16[4,6,3,2048]{3,0,2,1:T(4,128)(2,1)} copy(bf16[4,6,3,2048]{3,0,2,1:T(4,128)(2,1)} %bitcast.15) | data formatting | bytes 589824
  117.6 2.1 %copy.20 = bf16[4,12,6,1024]{3,0,2,1:T(4,128)(2,1)} copy(bf16[4,12,6,1024]{3,0,2,1:T(4,128)(2,1)} %bitcast.13) | data formatting | bytes 1179648
  119.7 1.4 %copy.21 = f32[16,759]{1,0:T(8,128)} copy(f32[16,759]{1,0:T(8,128)} %get-tuple-element.14) | data formatting | bytes 97152

commit v7 on v3

--- a/solution.py
+++ b/solution.py
@@ -42,13 +42,13 @@
 
 def quad_row(level, row, col):
     quad = 2 * (row // 6) + col // 3
-    return quad * SLAB + level * 18 + (row % 6) * 3 + col % 3
+    return quad * CELLS + level * 18 + (row % 6) * 3 + col % 3
 
 
 def orders():
-    natural = np.zeros((4 * SLAB, TOKENS), np.float32)
-    window = np.zeros((TOKENS, 4 * SLAB), np.float32)
-    merge = np.zeros((TOKENS, 4 * SLAB), np.float32)
+    natural = np.zeros((TOKENS, TOKENS), np.float32)
+    window = np.zeros((TOKENS, TOKENS), np.float32)
+    merge = np.zeros((TOKENS, TOKENS), np.float32)
     for level in range(4):
         for row in range(12):
             for col in range(6):
@@ -271,15 +271,19 @@
         return moves
 
     def fill(stage, order, values):
+        rows = dot(order[...], values)
         for quad in range(4):
-            rows = dot(order[quad * SLAB:(quad + 1) * SLAB, :], values).astype(BF16)
+            part = rows[quad * CELLS:(quad + 1) * CELLS]
+            part = jnp.concatenate([part[:, :WIDTH // 2], part[:, WIDTH // 2:]], axis=0).astype(BF16)
             if quad == 3:
-                landed[stage, quad] = rows
+                landed[stage, quad] = part
             else:
-                sent[stage, quad] = rows
+                sent[stage, quad] = part
 
     def arrived(stage, order):
-        return dot(order[...], landed[stage].reshape(4 * SLAB, WIDTH))
+        block = landed[stage].astype(F32)
+        rows = jnp.concatenate([block[:, :CELLS], block[:, CELLS:]], axis=2)
+        return dot(order[...], rows.reshape(TOKENS, WIDTH).astype(BF16))
 
     index_ref[...] = jnp.concatenate(
         [raw_index[...], jnp.zeros((WINDOW, 2 * LANES - WINDOW), jnp.int32)], axis=1
@@ -554,8 +558,8 @@
             pltpu.VMEM((WIDTH, WIDTH), BF16),
             pltpu.VMEM((RING, PIECE, OUT), BF16),
             pltpu.VMEM((TEAM, SLAB, OUT), BF16),
-            pltpu.VMEM((4, 3, SLAB, WIDTH), BF16),
-            pltpu.VMEM((4, 4, SLAB, WIDTH), BF16),
+            pltpu.VMEM((4, 3, 2 * CELLS, WIDTH // 2), BF16),
+            pltpu.VMEM((4, 4, 2 * CELLS, WIDTH // 2), BF16),
             pltpu.VMEM((TOKENS, WIDTH), BF16),
             pltpu.VMEM((TOKENS, WIDTH), BF16),
             pltpu.VMEM((TOKENS, 3 * WIDTH), BF16),

time: 118 us -> 116 us (0.983)
  Pallas kernels: 112 us -> 110 us
    pallas_call x1, Pallas kernels: 112 us -> 110 us  [fused(): pl.pallas_call(kernel, out_shape=(jax.ShapeDtypeStruct(cot.shape, BF16),...]
where the time goes in v7:
time: 116 us
  Pallas kernels  110 us (95%)
  local copies, waits for them, and re-layouts  5.35 us (5%)
    pallas_call x1, Pallas kernels, fused(): pl.pallas_call(kernel, out_shape=(jax.ShapeDtypeStruct(cot.shape, BF16),...  110 us
    unnamed x3, local copies, waits for them, and re-layouts  5.35 us

profile of v7, /device:TPU:1, one launch (start us, length us, event | category | flops | bytes accessed | tf_op | source)
XLA Modules:
  0.0 116.0 jit_solution(18120743869137414520)
XLA Ops:
  0.6 110.0 %fused_block.1 = (bf16[18,4,2048]{2,1,0:T(4,128)(2,1)}, bf16[72,4,1024]{2,1,0:T(4,128)(2,1)}, f32[16,759]{1,0:T(8,128)}) custom-call(bf16[288,288]{1,0:T(8,128)(2,1)} %constant.12.clone.nat2quad, bf16[288,288]{1,0:T(8,128)(2,1)} %constant.13.clone.quad2win, bf16[288,288]{1,0:T(8,128)(2,1)} %constant.14.clone.win2quad, ...), custom_call_target="tpu_custom_call" | custom-call | tf_op jit(solution)/shard_map/fused_block/pallas_call | solution.py:547
  110.7 1.8 %copy.19 = bf16[4,6,3,2048]{3,0,2,1:T(4,128)(2,1)} copy(bf16[4,6,3,2048]{3,0,2,1:T(4,128)(2,1)} %bitcast.15) | data formatting | bytes 589824
  112.5 2.1 %copy.20 = bf16[4,12,6,1024]{3,0,2,1:T(4,128)(2,1)} copy(bf16[4,12,6,1024]{3,0,2,1:T(4,128)(2,1)} %bitcast.13) | data formatting | bytes 1179648
  114.6 1.4 %copy.21 = f32[16,759]{1,0:T(8,128)} copy(f32[16,759]{1,0:T(8,128)} %get-tuple-element.14) | data formatting | bytes 97152
